TPU v7x, 256 devices: a whole 4x4x8 slice. The times are simulated.
256 devices in a mesh: grp: 16 (over y_lo, z), mem: 16 (over y_hi, x, core).
Axes of the slice: x: 4, y: 4 (y_hi: 2, y_lo: 2; y = y_hi * 2 + y_lo), z: 8, core: 2. Of those that a mesh axis runs over, the one named last changes fastest.
Arguments:
- obs_resid: float32 [131072, 64], P(('grp', 'mem')), may hold values from -6 to 6
- weight: float32 [131072, 64], P(('grp', 'mem')), may hold values from 0.1 to 10
- jac_src: float32 [5, 131072, 64], P(None, ('grp', 'mem')), may hold values from -6 to 6
- att_part: float32 [4, 131072, 64], P(None, ('grp', 'mem')), may hold values from -6 to 6
- seg_index: int32 [131072, 64], P(('grp', 'mem')), may hold values from 0 to 1023
- jac_cal: bfloat16 [131072, 64, 64], P(('grp', 'mem')), may hold values from -6 to 6
- cal_index: int32 [131072], P(('grp', 'mem')), may hold values from 0 to 16383, as said below
- block_count: int32 [256], P(('grp', 'mem')), may hold values from 1 to 512, 81920 in all
Outputs:
- src_update: float32 [5, 131072], P(None, ('grp', 'mem'))
- att_update: float32 [4, 1024], P(None, 'mem')
- cal_update: float32 [16384, 64], P(('grp', 'mem'))
- new_resid: float32 [131072, 64], P(('grp', 'mem'))
Inputs may be any that keep to these rules, and one draw needn't show every extreme that they name: `cal_index`: of the 512 source slots of one device, at most 4 have calibration blocks c with the same c // 64; some such share receives exactly 4 from every device.
All inputs are finite; a program needn't handle non-finite values. No bound on the sum of `block_count` on one device may be relied on, other than what follows from the above.
Results may differ from a plain program's by a relative error of at most 0.0003.
Values sent between devices are 32-bit elements; how exact they have to be, the bound alone decides.
No kernel may reach another device: no remote copies, remote signals or barrier semaphores. Data moves between devices by JAX's collectives and lax.ppermute only.
A program may use at most 64 MiB of HBM per device.

v0:
```python
import math

import jax
import jax.numpy as jnp
from jax import lax
from jax.sharding import PartitionSpec as P

CALB = 16384
CPAR = 64
KNOTS = 1024
OBS = 64


def knot_sums(terms, flat_seg):
    rows = flat_seg.shape[0]
    step_rows = math.gcd(rows, 2048)
    seg_blocks = flat_seg.reshape(rows // step_rows, step_rows)
    term_blocks = terms.reshape(terms.shape[0], rows // step_rows, step_rows).transpose(1, 0, 2)

    def one_block(carry, items):
        seg_part, term_part = items
        onehot = (seg_part[:, None] == jnp.arange(KNOTS, dtype=jnp.int32)[None, :]).astype(
            jnp.float32
        )
        return (carry + jnp.dot(term_part, onehot, precision=lax.Precision.HIGHEST), None)

    start = jnp.zeros((terms.shape[0], KNOTS), jnp.float32)
    total, unused = lax.scan(one_block, start, (seg_blocks, term_blocks))
    return total


def knot_lookup(table, flat_seg):
    rows = flat_seg.shape[0]
    step_rows = math.gcd(rows, 2048)
    seg_blocks = flat_seg.reshape(rows // step_rows, step_rows)

    def one_block(seg_part):
        onehot = (seg_part[:, None] == jnp.arange(KNOTS, dtype=jnp.int32)[None, :]).astype(
            jnp.float32
        )
        return lax.dot_general(
            table, onehot, (((1,), (1,)), ((), ())), precision=lax.Precision.HIGHEST
        )

    looked = lax.map(one_block, seg_blocks)
    return looked.transpose(1, 0, 2).reshape(table.shape[0], rows)


def body(obs_resid, weight, jac_src, att_part, seg_index, jac_cal, cal_index, block_count):
    nblock = obs_resid.shape[0]
    used = (jnp.arange(nblock, dtype=jnp.int32) < block_count[0]).astype(jnp.float32)
    live = weight * used[:, None]
    numer = jnp.sum(jac_src * (live * obs_resid)[None], axis=2)
    denom = 1.0 + jnp.sum(jac_src * jac_src * live[None], axis=2)
    src_update = numer / denom
    resid_one = obs_resid - jnp.sum(jac_src * src_update[:, :, None], axis=0)
    flat_seg = seg_index.reshape(-1)
    parts = att_part.reshape(4, -1)
    flat_live = live.reshape(-1)
    terms = jnp.concatenate(
        [parts * (flat_live * resid_one.reshape(-1))[None], parts * parts * flat_live[None]], axis=0
    )
    local_sums = knot_sums(terms, flat_seg)
    partial_value = lax.psum_scatter(local_sums, "mem", scatter_dimension=1, tiled=True)
    total = lax.psum(partial_value, "grp")
    att_out = total[:4] / (1.0 + total[4:])
    att_full = lax.all_gather(att_out, "mem", axis=1, tiled=True)
    looked = knot_lookup(att_full, flat_seg)
    new_resid = resid_one - jnp.sum(parts * looked, axis=0).reshape(nblock, OBS)
    jac_f = jac_cal.astype(jnp.float32)
    grad = jnp.einsum("brp,br->bp", jac_f, live * new_resid, precision=lax.Precision.HIGHEST)
    diag = jnp.einsum("brp,br->bp", jac_f * jac_f, live, precision=lax.Precision.HIGHEST)
    block_terms = jnp.concatenate([grad, diag], axis=1)
    groups = lax.axis_size("grp")
    members = lax.axis_size("mem")
    start = jnp.int32(0)
    inside = (cal_index >= start) & (
        cal_index < start + lax.axis_size(("grp", "mem")) * (CALB // (groups * members))
    )
    target = jnp.where(
        inside, cal_index, lax.axis_size(("grp", "mem")) * (CALB // (groups * members))
    )
    empty = jnp.zeros(
        (lax.axis_size(("grp", "mem")) * (CALB // (groups * members)), 2 * CPAR), jnp.float32
    )
    mine = lax.psum_scatter(
        empty.at[target].add(block_terms, mode="drop"),
        ("grp", "mem"),
        scatter_dimension=0,
        tiled=True,
    )
    cal_update = mine[:, :CPAR] / (1.0 + mine[:, CPAR:])
    return (src_update, att_out, cal_update, new_resid)


def solution(mesh):
    return jax.shard_map(
        body,
        mesh=mesh,
        in_specs=(
            P(("grp", "mem"), None),
            P(("grp", "mem"), None),
            P(None, ("grp", "mem"), None),
            P(None, ("grp", "mem"), None),
            P(("grp", "mem"), None),
            P(("grp", "mem"), None, None),
            P(("grp", "mem")),
            P(("grp", "mem")),
        ),
        out_specs=(
            P(None, ("grp", "mem")),
            P(None, "mem"),
            P(("grp", "mem"), None),
            P(("grp", "mem"), None),
        ),
        check_vma=False,
    )
```

profile of v0, /device:TPU:128, one launch (start us, length us, event | category | flops | bytes accessed | tf_op | source)
XLA Modules:
  0.0 1589.8 jit_solution(5112089669395651932)
XLA Ops:
  7.9 1.0 fusion.18
  8.9 0.1 copy.34
  9.0 1.2 multiply_reduce_fusion.2
  10.3 1.2 multiply_reduce_fusion.1
  11.4 0.9 sub.6
  12.4 0.1 copy.35
  12.5 0.1 reshape.68
  12.6 0.1 reshape.67
  12.7 1.0 copy.36
  13.8 0.1 reshape_reshape.4
  13.9 1.4 copy.33
  15.3 0.4 reshape.66
  15.7 0.1 broadcast_multiply_fusion
  15.9 45.3 %while.22 = (s32[]{:T(128)}, f32[8,1024]{1,0:T(8,128)S(1)}, f32[16,8,2048]{2,0,1:T(8,128)S(1)}, s32[16,2048]{1,0:T(8,128)S(1)}, s32[]{:T(128)}, /*index=5*/s32[]{:T(128)}) while((s32[]{:T(128)}, f32[8,1024]{1,0:T(8,128)S(1)}, f32[16,8,2048]{2,0,1:T(8,128)S(1)}, s32[16,2048]{1,0:T(8,128)S(1)}, s32[]{:T(128)}, ...), condition=%wide.region_4.5_spmd.clone, body=%wide.region_3.4_spmd.clone.sunk | while | flops 203440128 | bytes 286815 | solution.py:28
  16.0 2.7 fusion.26
  18.8 2.7 fusion.26
  21.6 2.7 fusion.26
  24.5 2.7 fusion.26
  27.3 2.7 fusion.26
  30.1 2.7 fusion.26
  33.0 2.7 fusion.26
  35.8 2.7 fusion.26
  38.6 2.7 fusion.26
  41.4 2.7 fusion.26
  44.3 2.7 fusion.26
  47.1 2.7 fusion.26
  49.9 2.7 fusion.26
  52.8 2.7 fusion.26
  55.6 2.7 fusion.26
  58.4 2.7 fusion.26
  61.2 1.0 copy.52
  62.3 74.6 %reduce-scatter.7.cloned.1.call-done = f32[64,8]{1,0:T(8,128)} async-done(((f32[1024,8]{1,0:T(8,128)}), f32[64,8]{1,0:T(8,128)}) %reduce-scatter.7.cloned.1.call-update) | async-done | bytes 2064
  136.9 0.8 copy.53
  137.7 27.8 %psum.7 = f32[8,64]{1,0:T(8,128)S(1)} all-reduce(f32[8,64]{1,0:T(8,128)S(1)} %copy.53), channel_id=1, replica_groups=mesh['grp'=16,'mem'=16] {'grp'}, use_global_device_ids=true, to_apply=%region_6.7 | all-reduce | flops 512 | bytes 4096 | tf_op jit(solution)/shard_map/psum | solution.py:65
  165.5 22.5 %all-gather = f32[16,64,4]{1,2,0:T(4,128)S(1)} all-gather(f32[1,64,4]{1,2,0:T(4,128)S(1)} %fusion.20), channel_id=1, replica_groups=mesh['grp'=16,'mem'=16] {'mem'}, dimensions={0}, use_global_device_ids=true | all-gather | bytes 17408 | tf_op jit(solution)/shard_map/all_gather | solution.py:67
  188.2 65.2 %while.21 = (s32[]{:T(128)}, f32[16,4,2048]{2,1,0:T(4,128)S(1)}, s32[16,2048]{1,0:T(8,128)S(1)}, f32[4,1024]{1,0:T(4,128)S(1)}, s32[]{:T(128)}) while((s32[]{:T(128)}, f32[16,4,2048]{2,1,0:T(4,128)S(1)}, s32[16,2048]{1,0:T(8,128)S(1)}, f32[4,1024]{1,0:T(4,128)S(1)}, s32[]{:T(128)}) %tuple.59), condition=%wide.region_8.9_spmd, body=%wide.region_7.8_spmd.sunk | while | flops 102760448 | bytes 73805 | solution.py:45
  188.2 4.0 fusion.25
  192.3 4.0 fusion.25
  196.3 4.0 fusion.25
  200.4 4.0 fusion.25
  204.5 4.0 fusion.25
  208.6 4.0 fusion.25
  212.6 4.0 fusion.25
  216.7 4.0 fusion.25
  220.8 4.0 fusion.25
  224.9 4.0 fusion.25
  228.9 4.0 fusion.25
  233.0 4.0 fusion.25
  237.1 4.0 fusion.25
  241.2 4.0 fusion.25
  245.3 4.0 fusion.25
  249.3 4.0 fusion.25
  253.4 0.3 copy.39
  253.7 0.4 reshape.69
  254.1 0.1 multiply_reduce_fusion
  254.2 0.1 copy.41
  254.4 0.7 fusion.17
  255.0 3.5 fusion.7
  258.5 0.1 copy.46
  258.6 0.1 copy.51
  258.8 6.1 scatter_custom_fusion
  264.9 0.6 add_divide_fusion.1
  265.5 1315.9 %reduce-scatter.5.cloned.1.call-done = f32[64,128]{1,0:T(8,128)} async-done(((f32[16384,128]{1,0:T(8,128)}), f32[64,128]{1,0:T(8,128)}) %reduce-scatter.5.cloned.1.call-update) | async-done | bytes 32784 | tf_op jit(solution)/shard_map/reduce_scatter | solution.py:86
  1581.4 1.5 fusion.15
  (66 shorter events, 1.8 us)
Async XLA Ops:
  7.2 129.7 %reduce-scatter.7.cloned.1.call-start = ((), (), s32[]{:S(2)}) async-start(), calls=%async_computation.3 | async-start | bytes 557056
  10.3 5.6 copy-start
  15.7 46.6 %copy-start.1 = (s32[512]{0:T(512)S(1)}, s32[512]{0:T(512)}, u32[]{:S(2)}) copy-start(s32[512]{0:T(512)} %param.18) | copy-start | bytes 6148
  62.2 1519.2 %reduce-scatter.5.cloned.1.call-start = ((), (), s32[]{:S(2)}) async-start(), calls=%async_computation.2 | async-start | bytes 8421376 | tf_op jit(solution)/shard_map/reduce_scatter | solution.py:86
Sparse Core Ops, SparseCore 0:
  62.3 74.5 reduce-scatter.6
  265.0 1316.3 reduce-scatter.4
where the time goes:
time: 1590 us
  waiting for transfers between devices  1390 us (87%)
  matrix products  109 us (7%)
  blocking collectives  50.4 us (3%)
  other arithmetic  17 us (1%)
    reduce_scatter x1, waiting for transfers between devices, body(): lax.psum_scatter(empty.at[target].add(block_terms, mode='drop'), ('grp',...  1320 us
    unnamed x3, waiting for transfers between devices  74.6 us
    dot_general x16, matrix products, one_block(): lax.dot_general(table, onehot, (((1,), (1,)), ((), ())), precision=lax.Pr...  64.8 us
    dot_general x16, matrix products, one_block(): jnp.dot(term_part, onehot, precision=lax.Precision.HIGHEST)  43.9 us
  transfers between devices with their start and end apart: 2, of which 2 were waited for; matrix products, arithmetic and copies ran while one was open for 0% of the time, Pallas kernels for 0%

commit v1 on v0

v1 whole, which is shorter than its diff:
```python
import jax
import jax.numpy as jnp
from jax import lax
from jax.experimental import pallas as pl
from jax.experimental.pallas import tpu as pltpu
from jax.sharding import PartitionSpec as P

CALB = 16384
CPAR = 64
KNOTS = 1024
OBS = 64
SLOTS = 4
AXES = ("grp", "mem")
F32 = jnp.float32
BF16 = jnp.bfloat16
VMEM = pl.BlockSpec(memory_space=pltpu.VMEM)
SMEM = pl.BlockSpec(memory_space=pltpu.SMEM)
ANY = pl.BlockSpec(memory_space=pl.ANY)
LIMIT = pltpu.CompilerParams(vmem_limit_bytes=48 * 1024 * 1024)
NT = (((1,), (1,)), ((), ()))
TN = (((0,), (0,)), ((), ()))


def halves(value):
    top = value.astype(BF16)
    return top, (value - top.astype(F32)).astype(BF16)


def source_kernel(count_ref, obs_ref, wt_ref, js_ref, ap_ref, seg_ref, upd_ref, resid_ref, sums_ref, terms):
    rows, slots = obs_ref.shape
    lane = lax.broadcasted_iota(jnp.int32, (1, slots), 1)
    used = (lane < count_ref[0]).astype(F32)
    live = wt_ref[...] * used
    obs = obs_ref[...]
    weighted = live * obs
    resid = obs
    for k in range(5):
        jac = js_ref[k]
        numer = jnp.sum(jac * weighted, axis=0, keepdims=True)
        denom = 1.0 + jnp.sum(jac * jac * live, axis=0, keepdims=True)
        update = numer / denom
        upd_ref[k : k + 1, :] = update
        resid = resid - jac * update
    resid_ref[...] = resid
    live_resid = live * resid
    for k in range(4):
        part = ap_ref[k]
        grad = part * live_resid
        diag = part * part * live
        for c in range(slots // 128):
            terms[c, pl.ds(k, rows, stride=8), :] = grad[:, 128 * c : 128 * c + 128]
            terms[c, pl.ds(4 + k, rows, stride=8), :] = diag[:, 128 * c : 128 * c + 128]
    ids = lax.broadcasted_iota(jnp.int32, (16, slots), 0).astype(F32).astype(BF16)
    batch = 4

    def step(i, total):
        left, right = [], []
        for b in range(batch):
            r = i * batch + b
            seg = seg_ref[pl.ds(r, 1), :]
            high = jnp.broadcast_to((seg >> 7).astype(F32), (16, slots)).astype(BF16)
            low = jnp.broadcast_to((seg & 127).astype(F32), (16, slots)).astype(BF16)
            place = pl.ds(pl.multiple_of(r * 8, 8), 8)
            value = jnp.concatenate([terms[c, place, :] for c in range(slots // 128)], axis=1)
            top = value.astype(BF16).astype(F32)
            both = jnp.concatenate([value, value - top], axis=0).astype(BF16)
            zero = jnp.zeros_like(both)
            one = jnp.ones_like(both)
            left.append(jnp.concatenate([jnp.where(high == jnp.asarray(h, BF16), both, zero) for h in range(8)], axis=0))
            right.append(jnp.concatenate([jnp.where(low == ids + jnp.asarray(16 * g, BF16), one, zero) for g in range(8)], axis=0))
        return total + lax.dot_general(
            jnp.concatenate(left, axis=1), jnp.concatenate(right, axis=1), NT, preferred_element_type=F32
        )

    total = lax.fori_loop(0, rows // batch, step, jnp.zeros((128, 128), F32))
    for h in range(8):
        sums_ref[8 * h : 8 * h + 8, :] = total[16 * h : 16 * h + 8] + total[16 * h + 8 : 16 * h + 16]


def slot_kernel(row_ref, column_ref, code_ref):
    slots = row_ref.shape[1]
    row = row_ref[...]
    owner = row >> 6
    before = lax.broadcasted_iota(jnp.int32, (slots, slots), 0) < lax.broadcasted_iota(jnp.int32, (slots, slots), 1)
    same = ((column_ref[...] >> 6) == owner) & before
    rank = jnp.sum(same.astype(F32), axis=0, keepdims=True)
    owner_f = owner.astype(F32)
    offset_f = (row & 63).astype(F32)
    for j in range(SLOTS):
        mine = rank == float(j)
        code_ref[j : j + 1, :] = jnp.where(mine, owner_f, -1.0)
        code_ref[SLOTS + j : SLOTS + j + 1, :] = jnp.where(mine, offset_f, 0.0)


def residual_kernel(
    count_ref, sums_ref, wt_ref, ap_ref, seg_ref, resid_ref, code_ref, jac_ref, out_ref, send_ref, jac_buf, vec_buf, live_buf, terms, sem
):
    rows, slots = wt_ref.shape
    copy = pltpu.make_async_copy(jac_ref, jac_buf, sem)
    copy.start()
    lane = lax.broadcasted_iota(jnp.int32, (1, slots), 1)
    used = (lane < count_ref[0]).astype(F32)
    live_buf[...] = wt_ref[...] * used
    tables = []
    for h in range(8):
        tile = sums_ref[8 * h : 8 * h + 8, :]
        tables.append(tile[0:4] / (1.0 + tile[4:8]))

    def look(i, carry):
        base = pl.multiple_of(i * 8, 8)
        for c in range(slots // 128):
            lanes = slice(128 * c, 128 * c + 128)
            seg = seg_ref[pl.ds(base, 8), lanes]
            low = seg & 127
            high = seg >> 7
            new = resid_ref[pl.ds(base, 8), lanes]
            masks = [high == h for h in range(8)]
            for k in range(4):
                found = jnp.zeros((8, 128), F32)
                for h in range(8):
                    table = jnp.broadcast_to(tables[h][k : k + 1, :], (8, 128))
                    found = jnp.where(masks[h], jnp.take_along_axis(table, low, axis=1), found)
                new = new - ap_ref[k, pl.ds(base, 8), lanes] * found
            out_ref[pl.ds(base, 8), lanes] = new
            vec_buf[pl.ds(base, 8), lanes] = new * live_buf[pl.ds(base, 8), lanes]
        return carry

    lax.fori_loop(0, rows // 8, look, 0)
    copy.wait()
    for c in range(slots // 128):
        lanes = slice(128 * c, 128 * c + 128)

        def blocks(i, carry):
            grad, diag = carry
            place = pl.ds(pl.multiple_of(i * 8, 8), 8)
            vec, live = vec_buf[place, lanes], live_buf[place, lanes]
            for b in range(8):
                jac = jac_buf[i * 8 + b, :, lanes].astype(F32)
                grad = grad + jac * vec[b : b + 1]
                diag = diag + jac * jac * live[b : b + 1]
            return grad, diag

        zero = jnp.zeros((CPAR, 128), F32)
        grad, diag = lax.fori_loop(0, rows // 8, blocks, (zero, zero))
        terms[0:CPAR, lanes] = grad
        terms[CPAR : 2 * CPAR, lanes] = diag
    top, rest = halves(terms[...])
    both = jnp.concatenate([top, rest], axis=0)
    owners = send_ref.shape[0]
    ids = lax.broadcasted_iota(jnp.int32, (owners, slots), 0).astype(F32).astype(BF16)
    one = jnp.ones((owners, slots), BF16)
    zero = jnp.zeros((owners, slots), BF16)
    anywhere = zero
    for j in range(SLOTS):
        code = jnp.broadcast_to(code_ref[j : j + 1, :], (owners, slots)).astype(BF16)
        pick = jnp.where(ids == code, one, zero)
        anywhere = anywhere + pick
        moved = lax.dot_general(pick, both, NT, preferred_element_type=F32)
        send_ref[:, 128 * j : 128 * j + 128] = moved[:, 0:128] + moved[:, 128:256]
    offsets = jnp.concatenate([code_ref[SLOTS : 2 * SLOTS, :], jnp.zeros((128 - SLOTS, slots), F32)], axis=0).astype(BF16)
    send_ref[:, 128 * SLOTS : 128 * SLOTS + 128] = lax.dot_general(anywhere, offsets, NT, preferred_element_type=F32)


def gather_kernel(got_ref, out_ref):
    devices = got_ref.shape[0]
    ids = lax.broadcasted_iota(jnp.int32, (devices, 64), 1).astype(F32)
    total = jnp.zeros((64, 256), F32)
    for j in range(SLOTS):
        offset = got_ref[:, 128 * SLOTS + j : 128 * SLOTS + j + 1]
        pick = (ids == offset).astype(F32).astype(BF16)
        top, rest = halves(got_ref[:, 128 * j : 128 * j + 128])
        total = total + lax.dot_general(pick, jnp.concatenate([top, rest], axis=1), TN, preferred_element_type=F32)
    sums = total[:, 0:128] + total[:, 128:256]
    out_ref[...] = sums[:, 0:CPAR] / (1.0 + sums[:, CPAR : 2 * CPAR])


def step_pairs(core, x, y, z):
    pairs = []
    for i in range(256):
        grp, mem = divmod(i, 16)
        c, px, py, pz = mem & 1, (mem >> 1) & 3, ((mem >> 3) << 1) | (grp >> 3), grp & 7
        c, px, py, pz = c ^ core, px ^ x, py ^ y, pz ^ z
        pairs.append((i, ((py & 1) * 8 + pz) * 16 + (py >> 1) * 8 + px * 2 + c))
    return pairs


def sum_everywhere(value):
    for step in ((1, 0, 0, 0), (0, 1, 0, 0), (0, 3, 0, 0), (0, 0, 1, 0), (0, 0, 3, 0), (0, 0, 0, 1), (0, 0, 0, 2), (0, 0, 0, 4)):
        value = value + lax.ppermute(value, AXES, step_pairs(*step))
    return value


def body(obs_resid, weight, jac_src, att_part, seg_index, jac_cal, cal_index, block_count):
    slots = obs_resid.shape[0]
    devices = lax.axis_size(AXES)
    obs, wt, seg = obs_resid.T, weight.T, seg_index.T
    js, ap = jac_src.transpose(0, 2, 1), att_part.transpose(0, 2, 1)
    jac = jac_cal.transpose(1, 2, 0)
    src_update, resid_one, sums = pl.pallas_call(
        source_kernel,
        out_shape=(
            jax.ShapeDtypeStruct((5, slots), F32),
            jax.ShapeDtypeStruct((OBS, slots), F32),
            jax.ShapeDtypeStruct((64, 128), F32),
        ),
        in_specs=[SMEM] + [VMEM] * 5,
        out_specs=(VMEM,) * 3,
        scratch_shapes=[pltpu.VMEM((slots // 128, OBS * 8, 128), F32)],
        compiler_params=LIMIT,
        name="source_step",
    )(block_count, obs, wt, js, ap, seg)
    code = pl.pallas_call(
        slot_kernel,
        out_shape=jax.ShapeDtypeStruct((2 * SLOTS, slots), F32),
        in_specs=[VMEM] * 2,
        out_specs=VMEM,
        compiler_params=LIMIT,
        name="slot_step",
    )(cal_index[None, :], cal_index[:, None])
    total = sum_everywhere(sums)
    new_resid, send = pl.pallas_call(
        residual_kernel,
        out_shape=(jax.ShapeDtypeStruct((OBS, slots), F32), jax.ShapeDtypeStruct((devices, 128 * (SLOTS + 1)), F32)),
        in_specs=[SMEM] + [VMEM] * 6 + [ANY],
        out_specs=(VMEM,) * 2,
        scratch_shapes=[
            pltpu.VMEM((OBS, CPAR, slots), BF16),
            pltpu.VMEM((OBS, slots), F32),
            pltpu.VMEM((OBS, slots), F32),
            pltpu.VMEM((2 * CPAR, slots), F32),
            pltpu.SemaphoreType.DMA,
        ],
        compiler_params=LIMIT,
        name="residual_step",
    )(block_count, total, wt, ap, seg, resid_one, code, jac)
    got = lax.all_to_all(send, AXES, 0, 0, tiled=True)
    cal_update = pl.pallas_call(
        gather_kernel,
        out_shape=jax.ShapeDtypeStruct((CALB // devices, CPAR), F32),
        in_specs=[VMEM],
        out_specs=VMEM,
        compiler_params=LIMIT,
        name="calibration_step",
    )(got)
    table = total.reshape(8, 8, 128)
    table = table[:, 0:4] / (1.0 + table[:, 4:8])
    mem = lax.axis_index("mem")
    att_out = lax.dynamic_slice(table, (mem // 2, 0, (mem % 2) * 64), (1, 4, 64))[0]
    return src_update, att_out, cal_update, new_resid.T


def solution(mesh):
    return jax.shard_map(
        body,
        mesh=mesh,
        in_specs=(
            P(AXES, None),
            P(AXES, None),
            P(None, AXES, None),
            P(None, AXES, None),
            P(AXES, None),
            P(AXES, None, None),
            P(AXES),
            P(AXES),
        ),
        out_specs=(P(None, AXES), P(None, "mem"), P(AXES, None), P(AXES, None)),
        check_vma=False,
    )
```

time: 1590 us -> 100 us (0.06)
  the two profiles are of different devices: /device:TPU:128 before, /device:TPU:1 now
where the time goes in v1:
time: 100 us; the launch traced here: 99.7 us
  waiting for transfers between devices  39.9 us (40%)
  starting transfers between devices  33.2 us (33%)
  local copies, waits for them, and re-layouts  13 us (13%)
  Pallas kernels  11.6 us (12%)
  between operations  1.42 us (1%)
    all_to_all x1, waiting for transfers between devices, body(): got = lax.all_to_all(send, AXES, 0, 0, tiled=True)  22.6 us
    all_to_all x1, starting transfers between devices, body(): got = lax.all_to_all(send, AXES, 0, 0, tiled=True)  21.1 us
    ppermute x8, waiting for transfers between devices, sum_everywhere(): value = value + lax.ppermute(value, AXES, step_pairs(*step))  17.3 us
    ppermute x8, starting transfers between devices, sum_everywhere(): value = value + lax.ppermute(value, AXES, step_pairs(*step))  12.1 us
    unnamed x21, local copies, waits for them, and re-layouts  10.6 us
    pallas_call x1, Pallas kernels, body(): pl.pallas_call(source_kernel, out_shape=(jax.ShapeDtypeStruct((5, slots),...  5.82 us
    pallas_call x1, Pallas kernels, body(): pl.pallas_call(residual_kernel, out_shape=(jax.ShapeDtypeStruct((OBS, slo...  4.45 us
  transfers between devices with their start and end apart: 9, of which 8 were waited for; matrix products, arithmetic and copies ran while one was open for 1% of the time, Pallas kernels for 0%

profile of v1, /device:TPU:1, one launch (start us, length us, event | category | flops | bytes accessed | tf_op | source)
XLA Modules:
  0.0 99.7 jit_solution(7815807918319904126)
XLA Ops:
  1.3 0.0 copy-start.1
  1.3 1.0 %copy-done.1 = f32[4,512,64]{1,2,0:T(8,128)S(1)} copy-done((f32[4,512,64]{1,2,0:T(8,128)S(1)}, f32[4,512,64]{1,2,0:T(8,128)}, u32[]{:S(2)}) %copy-start.1) | copy-done | bytes 524312
  2.3 0.0 copy-start.3
  2.3 1.1 %copy-done.3 = f32[5,512,64]{1,2,0:T(8,128)S(1)} copy-done((f32[5,512,64]{1,2,0:T(8,128)S(1)}, f32[5,512,64]{1,2,0:T(8,128)}, u32[]{:S(2)}) %copy-start.3) | copy-done | bytes 655384
  3.4 0.0 copy-start.4
  3.4 0.9 copy-done.4
  4.3 0.0 copy-start.6
  4.3 0.9 copy-done.6
  5.2 0.0 copy-start.8
  5.2 0.9 copy-done.8
  6.1 5.8 %source_step.1 = (f32[5,512]{1,0:T(8,128)}, f32[64,512]{1,0:T(8,128)S(1)}, f32[64,128]{1,0:T(8,128)S(1)}) custom-call(s32[1]{0:T(128)S(6)} %copy.18.count_ref, f32[64,512]{1,0:T(8,128)S(1)} %bitcast.27, f32[64,512]{1,0:T(8,128)S(1)} %bitcast.22, f32[5,64,512]{2,1,0:T(8,128)S(1)} %bitcast.20, f32[4,64,512]{2,1,0:T(8,128)S(1)} %bitcast.18, s32[64,512]{1,0:T(8,128)S(1)} %bitcast.24), custom_call_target="tpu_custom_call" | custom-call | tf_op jit(solution)/shard_map/source_step/pallas_call | solution.py:199
  11.9 3.2 %collective-permute-start = (f32[64,128]{1,0:T(8,128)S(1)}, f32[64,128]{1,0:T(8,128)S(1)}, u32[]{:S(2)}, u32[]{:S(2)}) collective-permute-start(f32[64,128]{1,0:T(8,128)S(1)} %get-tuple-element.10), channel_id=1, source_target_pairs={{0,1},{1,0},{2,3},{3,2},{4,5},{5,4},{6,7},{7,6},{8,9},{9,8},{10,11... | collective-permute-start | bytes 98312 | tf_op jit(solution)/shard_map/ppermute | solution.py:189
  15.2 0.9 collective-permute-done
  16.0 0.0 collective-permute-start.1
  16.0 2.8 %collective-permute-done.1 = f32[64,128]{1,0:T(8,128)S(1)} collective-permute-done((f32[64,128]{1,0:T(8,128)S(1)}, f32[64,128]{1,0:T(8,128)S(1)}, u32[]{:S(2)}, u32[]{:S(2)}) %collective-permute-start.1) | collective-permute-done | bytes 32800 | tf_op jit(solution)/shard_map/ppermute | solution.py:189
  18.8 0.8 collective-permute-start.2
  19.6 3.2 %collective-permute-done.2 = f32[64,128]{1,0:T(8,128)S(1)} collective-permute-done((f32[64,128]{1,0:T(8,128)S(1)}, f32[64,128]{1,0:T(8,128)S(1)}, u32[]{:S(2)}, u32[]{:S(2)}) %collective-permute-start.2) | collective-permute-done | bytes 32800 | tf_op jit(solution)/shard_map/ppermute | solution.py:189
  22.8 0.0 collective-permute-start.3
  22.8 2.8 %collective-permute-done.3 = f32[64,128]{1,0:T(8,128)S(1)} collective-permute-done((f32[64,128]{1,0:T(8,128)S(1)}, f32[64,128]{1,0:T(8,128)S(1)}, u32[]{:S(2)}, u32[]{:S(2)}) %collective-permute-start.3) | collective-permute-done | bytes 32800 | tf_op jit(solution)/shard_map/ppermute | solution.py:189
  25.6 1.1 %collective-permute-start.4 = (f32[64,128]{1,0:T(8,128)S(1)}, f32[64,128]{1,0:T(8,128)S(1)}, u32[]{:S(2)}, u32[]{:S(2)}) collective-permute-start(f32[64,128]{1,0:T(8,128)S(1)} %add.44), channel_id=1, source_target_pairs={{0,136},{1,137},{2,138},{3,139},{4,140},{5,141},{6,142},{7,143},{8... | collective-permute-start | bytes 98312 | tf_op jit(solution)/shard_map/ppermute | solution.py:189
  26.6 2.9 %collective-permute-done.4 = f32[64,128]{1,0:T(8,128)S(1)} collective-permute-done((f32[64,128]{1,0:T(8,128)S(1)}, f32[64,128]{1,0:T(8,128)S(1)}, u32[]{:S(2)}, u32[]{:S(2)}) %collective-permute-start.4) | collective-permute-done | bytes 32800 | tf_op jit(solution)/shard_map/ppermute | solution.py:189
  29.6 0.1 collective-permute-start.5
  29.6 2.7 %collective-permute-done.5 = f32[64,128]{1,0:T(8,128)S(1)} collective-permute-done((f32[64,128]{1,0:T(8,128)S(1)}, f32[64,128]{1,0:T(8,128)S(1)}, u32[]{:S(2)}, u32[]{:S(2)}) %collective-permute-start.5) | collective-permute-done | bytes 32800 | tf_op jit(solution)/shard_map/ppermute | solution.py:189
  32.3 1.6 %collective-permute-start.6 = (f32[64,128]{1,0:T(8,128)S(1)}, f32[64,128]{1,0:T(8,128)S(1)}, u32[]{:S(2)}, u32[]{:S(2)}) collective-permute-start(f32[64,128]{1,0:T(8,128)S(1)} %add.46), channel_id=1, source_target_pairs={{0,32},{1,33},{2,34},{3,35},{4,36},{5,37},{6,38},{7,39},{8,40},{9,... | collective-permute-start | bytes 98312 | tf_op jit(solution)/shard_map/ppermute | solution.py:189
  33.9 2.1 %collective-permute-done.6 = f32[64,128]{1,0:T(8,128)S(1)} collective-permute-done((f32[64,128]{1,0:T(8,128)S(1)}, f32[64,128]{1,0:T(8,128)S(1)}, u32[]{:S(2)}, u32[]{:S(2)}) %collective-permute-start.6) | collective-permute-done | bytes 32800 | tf_op jit(solution)/shard_map/ppermute | solution.py:189
  36.0 5.4 %collective-permute-start.7 = (f32[64,128]{1,0:T(8,128)S(1)}, f32[64,128]{1,0:T(8,128)S(1)}, u32[]{:S(2)}, u32[]{:S(2)}) collective-permute-start(f32[64,128]{1,0:T(8,128)S(1)} %add.47), channel_id=1, source_target_pairs={{0,64},{1,65},{2,66},{3,67},{4,68},{5,69},{6,70},{7,71},{8,72},{9,... | collective-permute-start | bytes 98312 | tf_op jit(solution)/shard_map/ppermute | solution.py:189
  41.3 0.8 copy.13.column_ref
  42.2 0.0 copy-start.9
  42.2 0.7 copy-done.9
  42.9 0.2 slot_step.1.code_ref
  43.0 0.0 collective-permute-done.7
  43.1 0.0 copy-start
  43.1 2.2 %copy-done = bf16[512,64,64]{0,2,1:T(8,128)(2,1)S(1)} copy-done((bf16[512,64,64]{0,2,1:T(8,128)(2,1)S(1)}, bf16[512,64,64]{0,2,1:T(8,128)(2,1)}, u32[]{:S(2)}) %copy-start) | copy-done | bytes 4194328
  45.2 0.0 copy-start.2
  45.2 1.0 %copy-done.2 = f32[4,512,64]{1,2,0:T(8,128)S(1)} copy-done((f32[4,512,64]{1,2,0:T(8,128)S(1)}, f32[4,512,64]{1,2,0:T(8,128)}, u32[]{:S(2)}) %copy-start.2) | copy-done | bytes 524312
  46.3 0.0 copy-start.5
  46.3 0.9 copy-done.5
  47.2 0.0 copy-start.7
  47.2 0.9 copy-done.7
  48.1 4.5 %residual_step.1 = (f32[64,512]{1,0:T(8,128)}, f32[256,640]{1,0:T(8,128)S(1)}) custom-call(s32[1]{0:T(128)S(6)} %copy.18.count_ref, f32[64,128]{1,0:T(8,128)S(1)} %add.48.sums_ref, f32[64,512]{1,0:T(8,128)S(1)} %bitcast.23, f32[4,64,512]{2,1,0:T(8,128)S(1)} %bitcast.19, s32[64,512]{1,0:T(8,128)S(1)} %bitcast.25, f32[64,512]{1,0:T(8,128)S(1)} %get-tuple-element.11.resid_ref, ...), custom_call_target="tpu_custom_call" | custom-call | tf_op jit(solution)/shard_map/residual_step/pallas_call | solution.py:221
  52.6 1.5 %copy.14 = f32[256,1,640]{2,1,0:T(1,128)} copy(f32[256,1,640]{2,0,1:T(8,128)S(1)} %bitcast.21) | data formatting | bytes 1310720 | tf_op jit(solution)/shard_map/all_to_all | solution.py:236
  54.1 21.1 %all-to-all-start = ((f32[256,1,640]{2,1,0:T(1,128)}), f32[256,1,640]{2,1,0:T(1,128)S(1)}, u32[]{:S(2)}, u32[]{:S(2)}) async-start(f32[256,1,640]{2,1,0:T(1,128)} %copy.14), calls=%async_computation | async-start | bytes 1310720 | tf_op jit(solution)/shard_map/all_to_all | solution.py:236
  75.3 0.7 fusion
  76.0 22.6 %all-to-all-done = f32[256,1,640]{2,1,0:T(1,128)S(1)} async-done(((f32[256,1,640]{2,1,0:T(1,128)}), f32[256,1,640]{2,1,0:T(1,128)S(1)}, u32[]{:S(2)}, u32[]{:S(2)}) %all-to-all-start) | async-done | bytes 655392 | tf_op jit(solution)/shard_map/all_to_all | solution.py:236
  98.6 1.1 %calibration_step.1 = f32[64,64]{1,0:T(8,128)} custom-call(f32[256,640]{1,0:T(8,128)S(1)} %bitcast.17), custom_call_target="tpu_custom_call" | custom-call | tf_op jit(solution)/shard_map/calibration_step/pallas_call | solution.py:237
  (10 shorter events, 0.1 us)
Async XLA Ops:
  1.3 1.0 %copy-start.1 = (f32[4,512,64]{1,2,0:T(8,128)S(1)}, f32[4,512,64]{1,2,0:T(8,128)}, u32[]{:S(2)}) copy-start(f32[4,512,64]{1,2,0:T(8,128)} %param.11) | copy-start | bytes 1572868
  2.3 1.1 %copy-start.3 = (f32[5,512,64]{1,2,0:T(8,128)S(1)}, f32[5,512,64]{1,2,0:T(8,128)}, u32[]{:S(2)}) copy-start(f32[5,512,64]{1,2,0:T(8,128)} %param.10) | copy-start | bytes 1966084
  3.4 0.9 copy-start.4
  4.3 0.9 copy-start.6
  5.2 0.9 copy-start.8
  11.9 4.1 %collective-permute-start = (f32[64,128]{1,0:T(8,128)S(1)}, f32[64,128]{1,0:T(8,128)S(1)}, u32[]{:S(2)}, u32[]{:S(2)}) collective-permute-start(f32[64,128]{1,0:T(8,128)S(1)} %get-tuple-element.10), channel_id=1, source_target_pairs={{0,1},{1,0},{2,3},{3,2},{4,5},{5,4},{6,7},{7,6},{8,9},{9,8},{10,11... | collective-permute-start | bytes 98312 | tf_op jit(solution)/shard_map/ppermute | solution.py:189
  16.0 2.8 %collective-permute-start.1 = (f32[64,128]{1,0:T(8,128)S(1)}, f32[64,128]{1,0:T(8,128)S(1)}, u32[]{:S(2)}, u32[]{:S(2)}) collective-permute-start(f32[64,128]{1,0:T(8,128)S(1)} %add.41), channel_id=1, source_target_pairs={{0,2},{1,3},{2,0},{3,1},{4,6},{5,7},{6,4},{7,5},{8,10},{9,11},{10,... | collective-permute-start | bytes 98312 | tf_op jit(solution)/shard_map/ppermute | solution.py:189
  18.8 4.0 %collective-permute-start.2 = (f32[64,128]{1,0:T(8,128)S(1)}, f32[64,128]{1,0:T(8,128)S(1)}, u32[]{:S(2)}, u32[]{:S(2)}) collective-permute-start(f32[64,128]{1,0:T(8,128)S(1)} %add.42), channel_id=1, source_target_pairs={{0,6},{1,7},{2,4},{3,5},{4,2},{5,3},{6,0},{7,1},{8,14},{9,15},{10,... | collective-permute-start | bytes 98312 | tf_op jit(solution)/shard_map/ppermute | solution.py:189
  22.8 2.8 %collective-permute-start.3 = (f32[64,128]{1,0:T(8,128)S(1)}, f32[64,128]{1,0:T(8,128)S(1)}, u32[]{:S(2)}, u32[]{:S(2)}) collective-permute-start(f32[64,128]{1,0:T(8,128)S(1)} %add.43), channel_id=1, source_target_pairs={{0,128},{1,129},{2,130},{3,131},{4,132},{5,133},{6,134},{7,135},{8... | collective-permute-start | bytes 98312 | tf_op jit(solution)/shard_map/ppermute | solution.py:189
  25.6 4.0 %collective-permute-start.4 = (f32[64,128]{1,0:T(8,128)S(1)}, f32[64,128]{1,0:T(8,128)S(1)}, u32[]{:S(2)}, u32[]{:S(2)}) collective-permute-start(f32[64,128]{1,0:T(8,128)S(1)} %add.44), channel_id=1, source_target_pairs={{0,136},{1,137},{2,138},{3,139},{4,140},{5,141},{6,142},{7,143},{8... | collective-permute-start | bytes 98312 | tf_op jit(solution)/shard_map/ppermute | solution.py:189
  29.6 2.8 %collective-permute-start.5 = (f32[64,128]{1,0:T(8,128)S(1)}, f32[64,128]{1,0:T(8,128)S(1)}, u32[]{:S(2)}, u32[]{:S(2)}) collective-permute-start(f32[64,128]{1,0:T(8,128)S(1)} %add.45), channel_id=1, source_target_pairs={{0,16},{1,17},{2,18},{3,19},{4,20},{5,21},{6,22},{7,23},{8,24},{9,... | collective-permute-start | bytes 98312 | tf_op jit(solution)/shard_map/ppermute | solution.py:189
  32.3 3.7 %collective-permute-start.6 = (f32[64,128]{1,0:T(8,128)S(1)}, f32[64,128]{1,0:T(8,128)S(1)}, u32[]{:S(2)}, u32[]{:S(2)}) collective-permute-start(f32[64,128]{1,0:T(8,128)S(1)} %add.46), channel_id=1, source_target_pairs={{0,32},{1,33},{2,34},{3,35},{4,36},{5,37},{6,38},{7,39},{8,40},{9,... | collective-permute-start | bytes 98312 | tf_op jit(solution)/shard_map/ppermute | solution.py:189
  36.0 7.0 %collective-permute-start.7 = (f32[64,128]{1,0:T(8,128)S(1)}, f32[64,128]{1,0:T(8,128)S(1)}, u32[]{:S(2)}, u32[]{:S(2)}) collective-permute-start(f32[64,128]{1,0:T(8,128)S(1)} %add.47), channel_id=1, source_target_pairs={{0,64},{1,65},{2,66},{3,67},{4,68},{5,69},{6,70},{7,71},{8,72},{9,... | collective-permute-start | bytes 98312 | tf_op jit(solution)/shard_map/ppermute | solution.py:189
  42.2 0.7 copy-start.9
  43.1 2.2 %copy-start = (bf16[512,64,64]{0,2,1:T(8,128)(2,1)S(1)}, bf16[512,64,64]{0,2,1:T(8,128)(2,1)}, u32[]{:S(2)}) copy-start(bf16[512,64,64]{0,2,1:T(8,128)(2,1)} %param.13) | copy-start | bytes 12582916
  45.2 1.0 %copy-start.2 = (f32[4,512,64]{1,2,0:T(8,128)S(1)}, f32[4,512,64]{1,2,0:T(8,128)}, u32[]{:S(2)}) copy-start(f32[4,512,64]{1,2,0:T(8,128)} %param.11) | copy-start | bytes 1572868
  46.3 0.9 copy-start.5
  47.2 0.9 copy-start.7
  54.1 44.5 %all-to-all-start = ((f32[256,1,640]{2,1,0:T(1,128)}), f32[256,1,640]{2,1,0:T(1,128)S(1)}, u32[]{:S(2)}, u32[]{:S(2)}) async-start(f32[256,1,640]{2,1,0:T(1,128)} %copy.14), calls=%async_computation | async-start | bytes 1310720 | tf_op jit(solution)/shard_map/all_to_all | solution.py:236

commit v2 on v1

v2 whole, which is shorter than its diff:
```python
import jax
import jax.numpy as jnp
from jax import lax
from jax.experimental import pallas as pl
from jax.experimental.pallas import tpu as pltpu
from jax.sharding import PartitionSpec as P

CALB = 16384
CPAR = 64
KNOTS = 1024
OBS = 64
SLOTS = 4
AXES = ("grp", "mem")
F32 = jnp.float32
BF16 = jnp.bfloat16
VMEM = pl.BlockSpec(memory_space=pltpu.VMEM)
SMEM = pl.BlockSpec(memory_space=pltpu.SMEM)
HBM = pl.BlockSpec(memory_space=pltpu.HBM)
LIMIT = pltpu.CompilerParams(vmem_limit_bytes=24 * 1024 * 1024)


def far(array):
    return pltpu.with_memory_space_constraint(array, pltpu.HBM)
NT = (((1,), (1,)), ((), ()))
TN = (((0,), (0,)), ((), ()))


def halves(value):
    top = value.astype(BF16)
    return top, (value - top.astype(F32)).astype(BF16)


def slots_of(row):
    slots = row.shape[1]
    owner = row >> 6
    column = jnp.broadcast_to(owner.astype(F32), (128, slots)).T[:, 0:1]
    before = lax.broadcasted_iota(jnp.int32, (slots, slots), 0) < lax.broadcasted_iota(jnp.int32, (slots, slots), 1)
    same = (column == owner.astype(F32)) & before
    rank = jnp.sum(same.astype(F32), axis=0, keepdims=True)
    offset = (row & 63).astype(F32)
    owners = [jnp.where(rank == float(j), owner.astype(F32), -1.0) for j in range(SLOTS)]
    return jnp.concatenate(owners + [jnp.where(rank == float(j), offset, 0.0) for j in range(SLOTS)], axis=0)


def source_kernel(
    count_ref, obs_hbm, wt_hbm, js_hbm, ap_hbm, seg_hbm,
    sums_ref, upd_ref, resid_ref,
    obs_ref, wt_ref, js_ref, ap_ref, seg_ref, terms, sems,
):
    pairs = ((obs_hbm, obs_ref), (wt_hbm, wt_ref), (js_hbm, js_ref), (ap_hbm, ap_ref), (seg_hbm, seg_ref))
    copies = [pltpu.make_async_copy(src, dst, sems.at[i]) for i, (src, dst) in enumerate(pairs)]
    for copy in copies:
        copy.start()
    for copy in copies[0:3]:
        copy.wait()
    rows, slots = obs_ref.shape
    lane = lax.broadcasted_iota(jnp.int32, (1, slots), 1)
    used = (lane < count_ref[0]).astype(F32)
    live = wt_ref[...] * used
    obs = obs_ref[...]
    weighted = live * obs
    resid = obs
    for k in range(5):
        jac = js_ref[k]
        numer = jnp.sum(jac * weighted, axis=0, keepdims=True)
        denom = 1.0 + jnp.sum(jac * jac * live, axis=0, keepdims=True)
        update = numer / denom
        upd_ref[k : k + 1, :] = update
        resid = resid - jac * update
    resid_ref[...] = resid
    copies[3].wait()
    copies[4].wait()
    live_resid = live * resid
    for k in range(4):
        part = ap_ref[k]
        grad = part * live_resid
        diag = part * part * live
        for c in range(slots // 128):
            terms[c, pl.ds(k, rows, stride=8), :] = grad[:, 128 * c : 128 * c + 128]
            terms[c, pl.ds(4 + k, rows, stride=8), :] = diag[:, 128 * c : 128 * c + 128]
    ids = lax.broadcasted_iota(jnp.int32, (16, slots), 0).astype(F32).astype(BF16)
    batch = 4

    def step(i, total):
        left, right = [], []
        for b in range(batch):
            r = i * batch + b
            seg = seg_ref[pl.ds(r, 1), :]
            high = jnp.broadcast_to((seg >> 7).astype(F32), (16, slots)).astype(BF16)
            low = jnp.broadcast_to((seg & 127).astype(F32), (16, slots)).astype(BF16)
            place = pl.ds(pl.multiple_of(r * 8, 8), 8)
            value = jnp.concatenate([terms[c, place, :] for c in range(slots // 128)], axis=1)
            top = value.astype(BF16).astype(F32)
            both = jnp.concatenate([value, value - top], axis=0).astype(BF16)
            zero = jnp.zeros_like(both)
            one = jnp.ones_like(both)
            left.append(jnp.concatenate([jnp.where(high == jnp.asarray(h, BF16), both, zero) for h in range(8)], axis=0))
            right.append(jnp.concatenate([jnp.where(low == ids + jnp.asarray(16 * g, BF16), one, zero) for g in range(8)], axis=0))
        return total + lax.dot_general(
            jnp.concatenate(left, axis=1), jnp.concatenate(right, axis=1), NT, preferred_element_type=F32
        )

    total = lax.fori_loop(0, rows // batch, step, jnp.zeros((128, 128), F32))
    for h in range(8):
        sums_ref[8 * h : 8 * h + 8, :] = total[16 * h : 16 * h + 8] + total[16 * h + 8 : 16 * h + 16]


def pick_rows(code_ref, j, owners):
    slots = code_ref.shape[1]
    ids = lax.broadcasted_iota(jnp.int32, (owners, slots), 0).astype(F32).astype(BF16)
    code = jnp.broadcast_to(code_ref[j : j + 1, :], (owners, slots)).astype(BF16)
    return jnp.where(ids == code, jnp.ones_like(code), jnp.zeros_like(code))


def near_kernel(count_ref, cal_ref, wt_hbm, ap_hbm, seg_hbm, jac_hbm, live_ref, ap_ref, seg_ref, jac_ref, code_ref, sems):
    pairs = ((wt_hbm, live_ref), (ap_hbm, ap_ref), (seg_hbm, seg_ref), (jac_hbm, jac_ref))
    copies = [pltpu.make_async_copy(src, dst, sems.at[i]) for i, (src, dst) in enumerate(pairs)]
    for copy in copies:
        copy.start()
    code_ref[...] = slots_of(cal_ref[...])
    copies[0].wait()
    lane = lax.broadcasted_iota(jnp.int32, (1, live_ref.shape[1]), 1)
    live_ref[...] = live_ref[...] * (lane < count_ref[0]).astype(F32)
    for copy in copies[1:]:
        copy.wait()


def early_kernel(live_ref, jac_ref, code_ref, send_ref, terms):
    rows, slots = live_ref.shape
    for c in range(slots // 128):
        lanes = slice(128 * c, 128 * c + 128)

        def blocks(i, diag):
            live = live_ref[pl.ds(pl.multiple_of(i * 8, 8), 8), lanes]
            for b in range(8):
                jac = jac_ref[i * 8 + b, :, lanes].astype(F32)
                diag = diag + jac * jac * live[b : b + 1]
            return diag

        terms[:, lanes] = lax.fori_loop(0, rows // 8, blocks, jnp.zeros((CPAR, 128), F32))
    top, rest = halves(terms[...])
    blank = jnp.zeros_like(top)
    both = jnp.concatenate([blank, top, blank, rest], axis=0)
    owners = send_ref.shape[0] // (SLOTS + 1)
    anywhere = jnp.zeros((owners, slots), BF16)
    for j in range(SLOTS):
        pick = pick_rows(code_ref, j, owners)
        anywhere = anywhere + pick
        moved = lax.dot_general(pick, both, NT, preferred_element_type=F32)
        send_ref[pl.ds(j, owners, stride=SLOTS + 1), :] = moved[:, 0:128] + moved[:, 128:256]
    offsets = jnp.concatenate([code_ref[SLOTS : 2 * SLOTS, :], jnp.zeros((128 - SLOTS, slots), F32)], axis=0).astype(BF16)
    moved = lax.dot_general(anywhere, offsets, NT, preferred_element_type=F32)
    send_ref[pl.ds(SLOTS, owners, stride=SLOTS + 1), :] = moved


def residual_kernel(
    place_ref, sums_ref, live_ref, ap_ref, seg_ref, jac_ref, resid_ref, code_ref, early_ref, att_ref, out_ref, send_ref, vec_buf, terms
):
    rows, slots = live_ref.shape
    tables = []
    for h in range(8):
        tile = sums_ref[8 * h : 8 * h + 8, :]
        tables.append(tile[0:4] / (1.0 + tile[4:8]))
    tile = sums_ref[pl.ds(pl.multiple_of((place_ref[0] // 2) * 8, 8), 8), :]
    mine = tile[0:4] / (1.0 + tile[4:8])
    att_ref[...] = jnp.where(lax.rem(place_ref[0], 2) == 0, mine[:, 0:64], mine[:, 64:128])

    def look(i, carry):
        base = pl.multiple_of(i * 8, 8)
        for c in range(slots // 128):
            lanes = slice(128 * c, 128 * c + 128)
            seg = seg_ref[pl.ds(base, 8), lanes]
            low = seg & 127
            high = seg >> 7
            new = resid_ref[pl.ds(base, 8), lanes]
            masks = [high == h for h in range(8)]
            for k in range(4):
                found = jnp.zeros((8, 128), F32)
                for h in range(8):
                    table = jnp.broadcast_to(tables[h][k : k + 1, :], (8, 128))
                    found = jnp.where(masks[h], jnp.take_along_axis(table, low, axis=1), found)
                new = new - ap_ref[k, pl.ds(base, 8), lanes] * found
            out_ref[pl.ds(base, 8), lanes] = new
            vec_buf[pl.ds(base, 8), lanes] = new * live_ref[pl.ds(base, 8), lanes]
        return carry

    lax.fori_loop(0, rows // 8, look, 0)
    for c in range(slots // 128):
        lanes = slice(128 * c, 128 * c + 128)

        def blocks(i, grad):
            vec = vec_buf[pl.ds(pl.multiple_of(i * 8, 8), 8), lanes]
            for b in range(8):
                grad = grad + jac_ref[i * 8 + b, :, lanes].astype(F32) * vec[b : b + 1]
            return grad

        terms[:, lanes] = lax.fori_loop(0, rows // 8, blocks, jnp.zeros((CPAR, 128), F32))
    top, rest = halves(terms[...])
    blank = jnp.zeros_like(top)
    both = jnp.concatenate([top, blank, rest, blank], axis=0)
    owners = send_ref.shape[0] // (SLOTS + 1)
    for j in range(SLOTS):
        moved = lax.dot_general(pick_rows(code_ref, j, owners), both, NT, preferred_element_type=F32)
        part = pl.ds(j, owners, stride=SLOTS + 1)
        send_ref[part, :] = early_ref[part, :] + moved[:, 0:128] + moved[:, 128:256]
    part = pl.ds(SLOTS, owners, stride=SLOTS + 1)
    send_ref[part, :] = early_ref[part, :]


def gather_kernel(got_ref, out_ref):
    devices = got_ref.shape[0] // (SLOTS + 1)
    ids = lax.broadcasted_iota(jnp.int32, (devices, 64), 1).astype(F32)
    offsets = got_ref[pl.ds(SLOTS, devices, stride=SLOTS + 1), :]
    total = jnp.zeros((64, 256), F32)
    for j in range(SLOTS):
        pick = (ids == offsets[:, j : j + 1]).astype(F32).astype(BF16)
        top, rest = halves(got_ref[pl.ds(j, devices, stride=SLOTS + 1), :])
        total = total + lax.dot_general(pick, jnp.concatenate([top, rest], axis=1), TN, preferred_element_type=F32)
    sums = total[:, 0:128] + total[:, 128:256]
    out_ref[...] = sums[:, 0:CPAR] / (1.0 + sums[:, CPAR : 2 * CPAR])


def step_pairs(core, x, y, z):
    pairs = []
    for i in range(256):
        grp, mem = divmod(i, 16)
        c, px, py, pz = mem & 1, (mem >> 1) & 3, ((mem >> 3) << 1) | (grp >> 3), grp & 7
        c, px, py, pz = c ^ core, px ^ x, py ^ y, pz ^ z
        pairs.append((i, ((py & 1) * 8 + pz) * 16 + (py >> 1) * 8 + px * 2 + c))
    return pairs


def moved(value, *step):
    return lax.ppermute(value, AXES, step_pairs(*step))


def body(obs_resid, weight, jac_src, att_part, seg_index, jac_cal, cal_index, block_count):
    slots = obs_resid.shape[0]
    devices = lax.axis_size(AXES)
    obs, wt, seg = far(obs_resid.T), far(weight.T), far(seg_index.T)
    js, ap = far(jac_src.transpose(0, 2, 1)), far(att_part.transpose(0, 2, 1))
    jac = far(jac_cal.transpose(1, 2, 0))
    plane = pltpu.VMEM((OBS, slots), F32)
    rows = pltpu.VMEM((devices * (SLOTS + 1), 128), F32)
    sums, src_update, resid_one = pl.pallas_call(
        source_kernel,
        out_shape=(pltpu.VMEM((64, 128), F32), jax.ShapeDtypeStruct((5, slots), F32), plane),
        in_specs=[SMEM] + [HBM] * 5,
        out_specs=(VMEM,) * 3,
        scratch_shapes=[
            pltpu.VMEM((OBS, slots), F32),
            pltpu.VMEM((OBS, slots), F32),
            pltpu.VMEM((5, OBS, slots), F32),
            pltpu.VMEM((4, OBS, slots), F32),
            pltpu.VMEM((OBS, slots), jnp.int32),
            pltpu.VMEM((slots // 128, OBS * 8, 128), F32),
            pltpu.SemaphoreType.DMA((5,)),
        ],
        compiler_params=LIMIT,
        name="source_step",
    )(block_count, obs, wt, js, ap, seg)
    live, near_ap, near_seg, near_jac, code = pl.pallas_call(
        near_kernel,
        out_shape=(
            plane,
            pltpu.VMEM((4, OBS, slots), F32),
            pltpu.VMEM((OBS, slots), jnp.int32),
            pltpu.VMEM((OBS, CPAR, slots), BF16),
            pltpu.VMEM((2 * SLOTS, slots), F32),
        ),
        in_specs=[SMEM, VMEM] + [HBM] * 4,
        out_specs=(VMEM,) * 5,
        scratch_shapes=[pltpu.SemaphoreType.DMA((4,))],
        compiler_params=LIMIT,
        name="near_step",
    )(block_count, cal_index[None, :], wt, ap, seg, jac)
    early = pl.pallas_call(
        early_kernel,
        out_shape=rows,
        in_specs=[VMEM] * 3,
        out_specs=VMEM,
        scratch_shapes=[pltpu.VMEM((CPAR, slots), F32)],
        compiler_params=LIMIT,
        name="early_step",
    )(live, near_jac, code)
    total = sums + moved(sums, 1, 0, 0, 0)
    total = (total + moved(total, 0, 1, 0, 0)) + (moved(total, 0, 2, 0, 0) + moved(total, 0, 3, 0, 0))
    total = (total + moved(total, 0, 0, 1, 0)) + (moved(total, 0, 0, 2, 0) + moved(total, 0, 0, 3, 0))
    total = total + moved(total, 0, 0, 0, 1)
    total = total + moved(total, 0, 0, 0, 2)
    total = total + moved(total, 0, 0, 0, 6)
    place = lax.axis_index("mem").astype(jnp.int32)[None]
    att_out, new_resid, send = pl.pallas_call(
        residual_kernel,
        out_shape=(
            jax.ShapeDtypeStruct((4, KNOTS // lax.axis_size("mem")), F32),
            jax.ShapeDtypeStruct((OBS, slots), F32),
            rows,
        ),
        in_specs=[SMEM] + [VMEM] * 8,
        out_specs=(VMEM,) * 3,
        scratch_shapes=[pltpu.VMEM((OBS, slots), F32), pltpu.VMEM((CPAR, slots), F32)],
        compiler_params=LIMIT,
        name="residual_step",
    )(place, total, live, near_ap, near_seg, near_jac, resid_one, code, early)
    got = lax.all_to_all(send.reshape(devices, 1, -1), AXES, 0, 0, tiled=True)
    cal_update = pl.pallas_call(
        gather_kernel,
        out_shape=jax.ShapeDtypeStruct((CALB // devices, CPAR), F32),
        in_specs=[VMEM],
        out_specs=VMEM,
        compiler_params=LIMIT,
        name="calibration_step",
    )(got.reshape(rows.shape))
    return src_update, att_out, cal_update, new_resid.T


def solution(mesh):
    return jax.shard_map(
        body,
        mesh=mesh,
        in_specs=(
            P(AXES, None),
            P(AXES, None),
            P(None, AXES, None),
            P(None, AXES, None),
            P(AXES, None),
            P(AXES, None, None),
            P(AXES),
            P(AXES),
        ),
        out_specs=(P(None, AXES), P(None, "mem"), P(AXES, None), P(AXES, None)),
        check_vma=False,
    )
```

time: 100 us -> 83.3 us (0.83)
  blocking collectives: 0 us -> 36.3 us
  waiting for transfers between devices: 39.9 us -> 8.98 us
  starting transfers between devices: 33.2 us -> 19.8 us
  local copies, waits for them, and re-layouts: 13 us -> 0.68 us
  Pallas kernels: 11.6 us -> 15.9 us
    all_to_all x0 -> x1, blocking collectives: none -> 36.3 us  [body(): got = lax.all_to_all(send.reshape(devices, 1, -1), AXES, 0, 0, tiled=True)]
    all_to_all x1 -> x0, waiting for transfers between devices: 22.6 us -> none  [body(): got = lax.all_to_all(send, AXES, 0, 0, tiled=True)]
    all_to_all x1 -> x0, starting transfers between devices: 21.1 us -> none  [body(): got = lax.all_to_all(send, AXES, 0, 0, tiled=True)]
    unnamed x21 -> x2, local copies, waits for them, and re-layouts: 10.6 us -> 0.68 us
    ppermute x8 -> x10, waiting for transfers between devices: 17.3 us -> 8.98 us  [moved(): return lax.ppermute(value, AXES, step_pairs(*step))]
    ppermute x8 -> x10, starting transfers between devices: 12.1 us -> 19.8 us  [moved(): return lax.ppermute(value, AXES, step_pairs(*step))]
    pallas_call x3 -> x4, Pallas kernels: 10.4 us -> 14.8 us  [the longest x1 7.14 us: body(): pl.pallas_call(source_kernel, out_shape=(pltpu.VMEM((64, 128), F32), jax....]
    all_to_all x1 -> x0, local copies, waits for them, and re-layouts: 1.55 us -> none  [body(): got = lax.all_to_all(send, AXES, 0, 0, tiled=True)]
  transfers between devices with their start and end apart: 9 -> 10, of which waited for: 8 -> 8; matrix products, arithmetic and copies ran while one was open for 1% -> 0% of each run, Pallas kernels for 0% -> 5%
where the time goes in v2:
time: 83.3 us; the launch traced here: 83.1 us
  blocking collectives  36.3 us (44%)
  starting transfers between devices  19.8 us (24%)
  Pallas kernels  15.9 us (19%)
  waiting for transfers between devices  8.98 us (11%)
  between operations  1.34 us (2%)
    all_to_all x1, blocking collectives, body(): got = lax.all_to_all(send.reshape(devices, 1, -1), AXES, 0, 0, tiled=True)  36.3 us
    ppermute x10, starting transfers between devices, moved(): return lax.ppermute(value, AXES, step_pairs(*step))  19.8 us
    ppermute x10, waiting for transfers between devices, moved(): return lax.ppermute(value, AXES, step_pairs(*step))  8.98 us
    pallas_call x1, Pallas kernels, body(): pl.pallas_call(source_kernel, out_shape=(pltpu.VMEM((64, 128), F32), jax....  7.14 us
    pallas_call x1, Pallas kernels, body(): pl.pallas_call(residual_kernel, out_shape=(jax.ShapeDtypeStruct((4, KNOTS...  3.43 us
    pallas_call x1, Pallas kernels, body(): pl.pallas_call(near_kernel, out_shape=(plane, pltpu.VMEM((4, OBS, slots),...  2.5 us
    pallas_call x1, Pallas kernels, body(): pl.pallas_call(early_kernel, out_shape=rows, in_specs=[VMEM] * 3, out_spe...  1.73 us
  transfers between devices with their start and end apart: 10, of which 8 were waited for; matrix products, arithmetic and copies ran while one was open for 0% of the time, Pallas kernels for 5%

profile of v2, /device:TPU:1, one launch (start us, length us, event | category | flops | bytes accessed | tf_op | source)
XLA Modules:
  0.0 83.1 jit_solution(10284617402288696568)
XLA Ops:
  1.3 7.1 %source_step.1 = (f32[64,128]{1,0:T(8,128)S(1)}, f32[5,512]{1,0:T(8,128)}, f32[64,512]{1,0:T(8,128)S(1)}) custom-call(s32[1]{0:T(128)S(6)} %copy.13.count_ref, f32[64,512]{1,0:T(8,128)} %bitcast.22, f32[64,512]{1,0:T(8,128)} %bitcast.18, f32[5,64,512]{2,1,0:T(8,128)} %bitcast.17, f32[4,64,512]{2,1,0:T(8,128)} %bitcast.15, s32[64,512]{1,0:T(8,128)} %bitcast.20), custom_call_target="tpu_custom_call" | custom-call | tf_op jit(solution)/shard_map/source_step/pallas_call | solution.py:245
  8.4 3.3 %collective-permute-start = (f32[64,128]{1,0:T(8,128)S(1)}, f32[64,128]{1,0:T(8,128)S(1)}, u32[]{:S(2)}, u32[]{:S(2)}) collective-permute-start(f32[64,128]{1,0:T(8,128)S(1)} %get-tuple-element.16), channel_id=1, source_target_pairs={{0,1},{1,0},{2,3},{3,2},{4,5},{5,4},{6,7},{7,6},{8,9},{9,8},{10,11... | collective-permute-start | bytes 98312 | tf_op jit(solution)/shard_map/ppermute | solution.py:234
  11.8 0.9 %collective-permute-done = f32[64,128]{1,0:T(8,128)S(1)} collective-permute-done((f32[64,128]{1,0:T(8,128)S(1)}, f32[64,128]{1,0:T(8,128)S(1)}, u32[]{:S(2)}, u32[]{:S(2)}) %collective-permute-start) | collective-permute-done | bytes 32800 | tf_op jit(solution)/shard_map/ppermute | solution.py:234
  12.6 0.8 collective-permute-start.3
  13.4 0.5 collective-permute-start.2
  13.9 2.0 %collective-permute-start.1 = (f32[64,128]{1,0:T(8,128)S(1)}, f32[64,128]{1,0:T(8,128)S(1)}, u32[]{:S(2)}, u32[]{:S(2)}) collective-permute-start(f32[64,128]{1,0:T(8,128)S(1)} %add.30), channel_id=1, source_target_pairs={{0,2},{1,3},{2,0},{3,1},{4,6},{5,7},{6,4},{7,5},{8,10},{9,11},{10,... | collective-permute-start | bytes 98312 | tf_op jit(solution)/shard_map/ppermute | solution.py:234
  15.9 0.7 collective-permute-done.3
  16.6 1.2 %collective-permute-done.2 = f32[64,128]{1,0:T(8,128)S(1)} collective-permute-done((f32[64,128]{1,0:T(8,128)S(1)}, f32[64,128]{1,0:T(8,128)S(1)}, u32[]{:S(2)}, u32[]{:S(2)}) %collective-permute-start.2) | collective-permute-done | bytes 32800 | tf_op jit(solution)/shard_map/ppermute | solution.py:234
  17.8 0.1 collective-permute-done.1
  17.9 2.6 %collective-permute-start.6 = (f32[64,128]{1,0:T(8,128)S(1)}, f32[64,128]{1,0:T(8,128)S(1)}, u32[]{:S(2)}, u32[]{:S(2)}) collective-permute-start(f32[64,128]{1,0:T(8,128)S(1)} %add_add_fusion.1), channel_id=1, source_target_pairs={{0,136},{1,137},{2,138},{3,139},{4,140},{5,141},{6,142},{7,143},{8... | collective-permute-start | bytes 98312 | tf_op jit(solution)/shard_map/ppermute | solution.py:234
  20.5 0.4 collective-permute-start.5
  20.8 0.3 collective-permute-start.4
  21.2 0.7 collective-permute-done.6
  21.9 2.8 %collective-permute-done.5 = f32[64,128]{1,0:T(8,128)S(1)} collective-permute-done((f32[64,128]{1,0:T(8,128)S(1)}, f32[64,128]{1,0:T(8,128)S(1)}, u32[]{:S(2)}, u32[]{:S(2)}) %collective-permute-start.5) | collective-permute-done | bytes 32800 | tf_op jit(solution)/shard_map/ppermute | solution.py:234
  24.8 0.0 collective-permute-done.4
  24.8 1.7 %collective-permute-start.7 = (f32[64,128]{1,0:T(8,128)S(1)}, f32[64,128]{1,0:T(8,128)S(1)}, u32[]{:S(2)}, u32[]{:S(2)}) collective-permute-start(f32[64,128]{1,0:T(8,128)S(1)} %add_add_fusion), channel_id=1, source_target_pairs={{0,16},{1,17},{2,18},{3,19},{4,20},{5,21},{6,22},{7,23},{8,24},{9,... | collective-permute-start | bytes 98312 | tf_op jit(solution)/shard_map/ppermute | solution.py:234
  26.5 1.3 %collective-permute-done.7 = f32[64,128]{1,0:T(8,128)S(1)} collective-permute-done((f32[64,128]{1,0:T(8,128)S(1)}, f32[64,128]{1,0:T(8,128)S(1)}, u32[]{:S(2)}, u32[]{:S(2)}) %collective-permute-start.7) | collective-permute-done | bytes 32800 | tf_op jit(solution)/shard_map/ppermute | solution.py:234
  27.8 3.0 %collective-permute-start.8 = (f32[64,128]{1,0:T(8,128)S(1)}, f32[64,128]{1,0:T(8,128)S(1)}, u32[]{:S(2)}, u32[]{:S(2)}) collective-permute-start(f32[64,128]{1,0:T(8,128)S(1)} %add.37), channel_id=1, source_target_pairs={{0,32},{1,33},{2,34},{3,35},{4,36},{5,37},{6,38},{7,39},{8,40},{9,... | collective-permute-start | bytes 98312 | tf_op jit(solution)/shard_map/ppermute | solution.py:234
  30.8 1.3 %collective-permute-done.8 = f32[64,128]{1,0:T(8,128)S(1)} collective-permute-done((f32[64,128]{1,0:T(8,128)S(1)}, f32[64,128]{1,0:T(8,128)S(1)}, u32[]{:S(2)}, u32[]{:S(2)}) %collective-permute-start.8) | collective-permute-done | bytes 32800 | tf_op jit(solution)/shard_map/ppermute | solution.py:234
  32.1 5.2 %collective-permute-start.9 = (f32[64,128]{1,0:T(8,128)S(1)}, f32[64,128]{1,0:T(8,128)S(1)}, u32[]{:S(2)}, u32[]{:S(2)}) collective-permute-start(f32[64,128]{1,0:T(8,128)S(1)} %add.38), channel_id=1, source_target_pairs={{0,96},{1,97},{2,98},{3,99},{4,100},{5,101},{6,102},{7,103},{8,104... | collective-permute-start | bytes 98312 | tf_op jit(solution)/shard_map/ppermute | solution.py:234
  37.3 0.0 copy-start
  37.3 0.7 copy-done
  38.0 2.5 %near_step.1 = (f32[64,512]{1,0:T(8,128)S(1)}, f32[4,64,512]{2,1,0:T(8,128)S(1)}, s32[64,512]{1,0:T(8,128)S(1)}, bf16[64,64,512]{2,1,0:T(8,128)(2,1)S(1)}, f32[8,512]{1,0:T(8,128)S(1)}) custom-call(s32[1]{0:T(128)S(6)} %copy.13.count_ref, s32[1,512]{1,0:T(1,128)S(1)} %bitcast.13, f32[64,512]{1,0:T(8,128)} %bitcast.19, f32[4,64,512]{2,1,0:T(8,128)} %bitcast.16, ...), custom_call_target="tpu_custom_call" | custom-call | tf_op jit(solution)/shard_map/near_step/pallas_call | solution.py:262
  40.5 1.7 %early_step.1.early_ref = f32[1280,128]{1,0:T(8,128)S(1)} custom-call(f32[64,512]{1,0:T(8,128)S(1)} %get-tuple-element.17.live_ref, bf16[64,64,512]{2,1,0:T(8,128)(2,1)S(1)} %get-tuple-element.20.jac_ref, f32[8,512]{1,0:T(8,128)S(1)} %get-tuple-element.22.code_ref), custom_call_target="tpu_custom_call" | custom-call | tf_op jit(solution)/shard_map/early_step/pallas_call | solution.py:277
  42.2 0.0 collective-permute-done.9
  42.2 3.4 %residual_step.1 = (f32[4,64]{1,0:T(4,128)}, f32[64,512]{1,0:T(8,128)}, f32[1280,128]{1,0:T(8,128)S(1)}) custom-call(s32[1]{0:T(128)} %bitcast.5.place_ref, f32[64,128]{1,0:T(8,128)S(1)} %add.39.sums_ref, f32[64,512]{1,0:T(8,128)S(1)} %get-tuple-element.17.live_ref, f32[4,64,512]{2,1,0:T(8,128)S(1)} %get-tuple-element.18.ap_ref, ...), custom_call_target="tpu_custom_call" | custom-call | tf_op jit(solution)/shard_map/residual_step/pallas_call | solution.py:293
  45.7 36.3 %all_to_all.5 = f32[256,1,640]{2,1,0:T(1,128)S(1)} all-to-all(f32[256,1,640]{2,1,0:T(1,128)S(1)} %bitcast.12), channel_id=1, replica_groups=mesh['grp'=16,'mem'=16] {'grp','mem'}, dimensions={0} | all-to-all | bytes 1310720 | tf_op jit(solution)/shard_map/all_to_all | solution.py:306
  82.0 1.1 %calibration_step.1 = f32[64,64]{1,0:T(8,128)} custom-call(f32[1280,128]{1,0:T(8,128)S(1)} %bitcast.11), custom_call_target="tpu_custom_call" | custom-call | tf_op jit(solution)/shard_map/calibration_step/pallas_call | solution.py:307
  (6 shorter events, 0.0 us)
Async XLA Ops:
  8.4 4.2 %collective-permute-start = (f32[64,128]{1,0:T(8,128)S(1)}, f32[64,128]{1,0:T(8,128)S(1)}, u32[]{:S(2)}, u32[]{:S(2)}) collective-permute-start(f32[64,128]{1,0:T(8,128)S(1)} %get-tuple-element.16), channel_id=1, source_target_pairs={{0,1},{1,0},{2,3},{3,2},{4,5},{5,4},{6,7},{7,6},{8,9},{9,8},{10,11... | collective-permute-start | bytes 98312 | tf_op jit(solution)/shard_map/ppermute | solution.py:234
  12.6 4.0 %collective-permute-start.3 = (f32[64,128]{1,0:T(8,128)S(1)}, f32[64,128]{1,0:T(8,128)S(1)}, u32[]{:S(2)}, u32[]{:S(2)}) collective-permute-start(f32[64,128]{1,0:T(8,128)S(1)} %add.30), channel_id=1, source_target_pairs={{0,6},{1,7},{2,4},{3,5},{4,2},{5,3},{6,0},{7,1},{8,14},{9,15},{10,... | collective-permute-start | bytes 98312 | tf_op jit(solution)/shard_map/ppermute | solution.py:234
  13.4 4.4 %collective-permute-start.2 = (f32[64,128]{1,0:T(8,128)S(1)}, f32[64,128]{1,0:T(8,128)S(1)}, u32[]{:S(2)}, u32[]{:S(2)}) collective-permute-start(f32[64,128]{1,0:T(8,128)S(1)} %add.30), channel_id=1, source_target_pairs={{0,4},{1,5},{2,6},{3,7},{4,0},{5,1},{6,2},{7,3},{8,12},{9,13},{10,... | collective-permute-start | bytes 98312 | tf_op jit(solution)/shard_map/ppermute | solution.py:234
  13.9 4.0 %collective-permute-start.1 = (f32[64,128]{1,0:T(8,128)S(1)}, f32[64,128]{1,0:T(8,128)S(1)}, u32[]{:S(2)}, u32[]{:S(2)}) collective-permute-start(f32[64,128]{1,0:T(8,128)S(1)} %add.30), channel_id=1, source_target_pairs={{0,2},{1,3},{2,0},{3,1},{4,6},{5,7},{6,4},{7,5},{8,10},{9,11},{10,... | collective-permute-start | bytes 98312 | tf_op jit(solution)/shard_map/ppermute | solution.py:234
  17.9 4.1 %collective-permute-start.6 = (f32[64,128]{1,0:T(8,128)S(1)}, f32[64,128]{1,0:T(8,128)S(1)}, u32[]{:S(2)}, u32[]{:S(2)}) collective-permute-start(f32[64,128]{1,0:T(8,128)S(1)} %add_add_fusion.1), channel_id=1, source_target_pairs={{0,136},{1,137},{2,138},{3,139},{4,140},{5,141},{6,142},{7,143},{8... | collective-permute-start | bytes 98312 | tf_op jit(solution)/shard_map/ppermute | solution.py:234
  20.5 4.3 %collective-permute-start.5 = (f32[64,128]{1,0:T(8,128)S(1)}, f32[64,128]{1,0:T(8,128)S(1)}, u32[]{:S(2)}, u32[]{:S(2)}) collective-permute-start(f32[64,128]{1,0:T(8,128)S(1)} %add_add_fusion.1), channel_id=1, source_target_pairs={{0,8},{1,9},{2,10},{3,11},{4,12},{5,13},{6,14},{7,15},{8,0},{9,1},... | collective-permute-start | bytes 98312 | tf_op jit(solution)/shard_map/ppermute | solution.py:234
  20.8 3.9 %collective-permute-start.4 = (f32[64,128]{1,0:T(8,128)S(1)}, f32[64,128]{1,0:T(8,128)S(1)}, u32[]{:S(2)}, u32[]{:S(2)}) collective-permute-start(f32[64,128]{1,0:T(8,128)S(1)} %add_add_fusion.1), channel_id=1, source_target_pairs={{0,128},{1,129},{2,130},{3,131},{4,132},{5,133},{6,134},{7,135},{8... | collective-permute-start | bytes 98312 | tf_op jit(solution)/shard_map/ppermute | solution.py:234
  24.8 3.0 %collective-permute-start.7 = (f32[64,128]{1,0:T(8,128)S(1)}, f32[64,128]{1,0:T(8,128)S(1)}, u32[]{:S(2)}, u32[]{:S(2)}) collective-permute-start(f32[64,128]{1,0:T(8,128)S(1)} %add_add_fusion), channel_id=1, source_target_pairs={{0,16},{1,17},{2,18},{3,19},{4,20},{5,21},{6,22},{7,23},{8,24},{9,... | collective-permute-start | bytes 98312 | tf_op jit(solution)/shard_map/ppermute | solution.py:234
  27.8 4.3 %collective-permute-start.8 = (f32[64,128]{1,0:T(8,128)S(1)}, f32[64,128]{1,0:T(8,128)S(1)}, u32[]{:S(2)}, u32[]{:S(2)}) collective-permute-start(f32[64,128]{1,0:T(8,128)S(1)} %add.37), channel_id=1, source_target_pairs={{0,32},{1,33},{2,34},{3,35},{4,36},{5,37},{6,38},{7,39},{8,40},{9,... | collective-permute-start | bytes 98312 | tf_op jit(solution)/shard_map/ppermute | solution.py:234
  32.1 10.1 %collective-permute-start.9 = (f32[64,128]{1,0:T(8,128)S(1)}, f32[64,128]{1,0:T(8,128)S(1)}, u32[]{:S(2)}, u32[]{:S(2)}) collective-permute-start(f32[64,128]{1,0:T(8,128)S(1)} %add.38), channel_id=1, source_target_pairs={{0,96},{1,97},{2,98},{3,99},{4,100},{5,101},{6,102},{7,103},{8,104... | collective-permute-start | bytes 98312 | tf_op jit(solution)/shard_map/ppermute | solution.py:234
  37.3 0.7 copy-start

commit v3 on v2

--- a/solution.py
+++ b/solution.py
@@ -79,28 +79,19 @@
             terms[c, pl.ds(k, rows, stride=8), :] = grad[:, 128 * c : 128 * c + 128]
             terms[c, pl.ds(4 + k, rows, stride=8), :] = diag[:, 128 * c : 128 * c + 128]
     ids = lax.broadcasted_iota(jnp.int32, (16, slots), 0).astype(F32).astype(BF16)
-    batch = 4
-
-    def step(i, total):
-        left, right = [], []
-        for b in range(batch):
-            r = i * batch + b
-            seg = seg_ref[pl.ds(r, 1), :]
-            high = jnp.broadcast_to((seg >> 7).astype(F32), (16, slots)).astype(BF16)
-            low = jnp.broadcast_to((seg & 127).astype(F32), (16, slots)).astype(BF16)
-            place = pl.ds(pl.multiple_of(r * 8, 8), 8)
-            value = jnp.concatenate([terms[c, place, :] for c in range(slots // 128)], axis=1)
-            top = value.astype(BF16).astype(F32)
-            both = jnp.concatenate([value, value - top], axis=0).astype(BF16)
-            zero = jnp.zeros_like(both)
-            one = jnp.ones_like(both)
-            left.append(jnp.concatenate([jnp.where(high == jnp.asarray(h, BF16), both, zero) for h in range(8)], axis=0))
-            right.append(jnp.concatenate([jnp.where(low == ids + jnp.asarray(16 * g, BF16), one, zero) for g in range(8)], axis=0))
-        return total + lax.dot_general(
-            jnp.concatenate(left, axis=1), jnp.concatenate(right, axis=1), NT, preferred_element_type=F32
-        )
-
-    total = lax.fori_loop(0, rows // batch, step, jnp.zeros((128, 128), F32))
+    left, right = [], []
+    for r in range(rows):
+        seg = seg_ref[r : r + 1, :]
+        high = jnp.broadcast_to((seg >> 7).astype(F32), (16, slots)).astype(BF16)
+        low = jnp.broadcast_to((seg & 127).astype(F32), (16, slots)).astype(BF16)
+        value = jnp.concatenate([terms[c, 8 * r : 8 * r + 8, :] for c in range(slots // 128)], axis=1)
+        top = value.astype(BF16).astype(F32)
+        both = jnp.concatenate([value, value - top], axis=0).astype(BF16)
+        zero = jnp.zeros_like(both)
+        one = jnp.ones_like(both)
+        left.append(jnp.concatenate([jnp.where(high == jnp.asarray(h, BF16), both, zero) for h in range(8)], axis=0))
+        right.append(jnp.concatenate([jnp.where(low == ids + jnp.asarray(16 * g, BF16), one, zero) for g in range(8)], axis=0))
+    total = lax.dot_general(jnp.concatenate(left, axis=1), jnp.concatenate(right, axis=1), NT, preferred_element_type=F32)
     for h in range(8):
         sums_ref[8 * h : 8 * h + 8, :] = total[16 * h : 16 * h + 8] + total[16 * h + 8 : 16 * h + 16]
 
@@ -112,32 +103,31 @@
     return jnp.where(ids == code, jnp.ones_like(code), jnp.zeros_like(code))
 
 
-def near_kernel(count_ref, cal_ref, wt_hbm, ap_hbm, seg_hbm, jac_hbm, live_ref, ap_ref, seg_ref, jac_ref, code_ref, sems):
-    pairs = ((wt_hbm, live_ref), (ap_hbm, ap_ref), (seg_hbm, seg_ref), (jac_hbm, jac_ref))
+def near_kernel(
+    count_ref, cal_hbm, wt_hbm, ap_hbm, seg_hbm, jac_hbm, live_ref, ap_ref, seg_ref, jac_ref, code_ref, send_ref, cal_ref, terms, sems
+):
+    rows, slots = live_ref.shape
+    step = rows // 4
+    pairs = [(cal_hbm, cal_ref), (wt_hbm, live_ref)]
+    pairs += [(jac_hbm.at[pl.ds(step * q, step)], jac_ref.at[pl.ds(step * q, step)]) for q in range(4)]
+    pairs += [(ap_hbm, ap_ref), (seg_hbm, seg_ref)]
     copies = [pltpu.make_async_copy(src, dst, sems.at[i]) for i, (src, dst) in enumerate(pairs)]
     for copy in copies:
         copy.start()
+    copies[0].wait()
     code_ref[...] = slots_of(cal_ref[...])
-    copies[0].wait()
-    lane = lax.broadcasted_iota(jnp.int32, (1, live_ref.shape[1]), 1)
+    copies[1].wait()
+    lane = lax.broadcasted_iota(jnp.int32, (1, slots), 1)
     live_ref[...] = live_ref[...] * (lane < count_ref[0]).astype(F32)
-    for copy in copies[1:]:
-        copy.wait()
-
-
-def early_kernel(live_ref, jac_ref, code_ref, send_ref, terms):
-    rows, slots = live_ref.shape
-    for c in range(slots // 128):
-        lanes = slice(128 * c, 128 * c + 128)
-
-        def blocks(i, diag):
-            live = live_ref[pl.ds(pl.multiple_of(i * 8, 8), 8), lanes]
-            for b in range(8):
-                jac = jac_ref[i * 8 + b, :, lanes].astype(F32)
-                diag = diag + jac * jac * live[b : b + 1]
-            return diag
-
-        terms[:, lanes] = lax.fori_loop(0, rows // 8, blocks, jnp.zeros((CPAR, 128), F32))
+    for q in range(4):
+        copies[2 + q].wait()
+        for c in range(slots // 128):
+            lanes = slice(128 * c, 128 * c + 128)
+            diag = jnp.zeros((CPAR, 128), F32) if q == 0 else terms[:, lanes]
+            for r in range(step * q, step * q + step):
+                jac = jac_ref[r, :, lanes].astype(F32)
+                diag = diag + jac * jac * live_ref[r : r + 1, lanes]
+            terms[:, lanes] = diag
     top, rest = halves(terms[...])
     blank = jnp.zeros_like(top)
     both = jnp.concatenate([blank, top, blank, rest], axis=0)
@@ -151,40 +141,38 @@
     offsets = jnp.concatenate([code_ref[SLOTS : 2 * SLOTS, :], jnp.zeros((128 - SLOTS, slots), F32)], axis=0).astype(BF16)
     moved = lax.dot_general(anywhere, offsets, NT, preferred_element_type=F32)
     send_ref[pl.ds(SLOTS, owners, stride=SLOTS + 1), :] = moved
+    for copy in copies[6:]:
+        copy.wait()
 
 
 def residual_kernel(
-    place_ref, sums_ref, live_ref, ap_ref, seg_ref, jac_ref, resid_ref, code_ref, early_ref, att_ref, out_ref, send_ref, vec_buf, terms
+    sums_ref, live_ref, ap_ref, seg_ref, jac_ref, resid_ref, code_ref, early_ref, att_ref, out_ref, send_ref, vec_buf, terms
 ):
     rows, slots = live_ref.shape
     tables = []
     for h in range(8):
         tile = sums_ref[8 * h : 8 * h + 8, :]
         tables.append(tile[0:4] / (1.0 + tile[4:8]))
-    tile = sums_ref[pl.ds(pl.multiple_of((place_ref[0] // 2) * 8, 8), 8), :]
+    place = lax.axis_index("mem")
+    tile = sums_ref[pl.ds(pl.multiple_of((place // 2) * 8, 8), 8), :]
     mine = tile[0:4] / (1.0 + tile[4:8])
-    att_ref[...] = jnp.where(lax.rem(place_ref[0], 2) == 0, mine[:, 0:64], mine[:, 64:128])
-
-    def look(i, carry):
-        base = pl.multiple_of(i * 8, 8)
+    att_ref[...] = jnp.where(lax.rem(place, 2) == 0, mine[:, 0:64], mine[:, 64:128])
+
+    for i in range(rows // 8):
+        block = slice(8 * i, 8 * i + 8)
         for c in range(slots // 128):
             lanes = slice(128 * c, 128 * c + 128)
-            seg = seg_ref[pl.ds(base, 8), lanes]
+            seg = seg_ref[block, lanes]
             low = seg & 127
-            high = seg >> 7
-            new = resid_ref[pl.ds(base, 8), lanes]
-            masks = [high == h for h in range(8)]
+            bits = [(seg & (128 << n)) != 0 for n in range(3)]
+            new = resid_ref[block, lanes]
             for k in range(4):
-                found = jnp.zeros((8, 128), F32)
-                for h in range(8):
-                    table = jnp.broadcast_to(tables[h][k : k + 1, :], (8, 128))
-                    found = jnp.where(masks[h], jnp.take_along_axis(table, low, axis=1), found)
-                new = new - ap_ref[k, pl.ds(base, 8), lanes] * found
-            out_ref[pl.ds(base, 8), lanes] = new
-            vec_buf[pl.ds(base, 8), lanes] = new * live_ref[pl.ds(base, 8), lanes]
-        return carry
-
-    lax.fori_loop(0, rows // 8, look, 0)
+                found = [jnp.take_along_axis(jnp.broadcast_to(table[k : k + 1, :], (8, 128)), low, axis=1) for table in tables]
+                for bit in bits:
+                    found = [jnp.where(bit, odd, even) for even, odd in zip(found[0::2], found[1::2])]
+                new = new - ap_ref[k, block, lanes] * found[0]
+            out_ref[block, lanes] = new
+            vec_buf[block, lanes] = new * live_ref[block, lanes]
     for c in range(slots // 128):
         lanes = slice(128 * c, 128 * c + 128)
 
@@ -194,7 +182,7 @@
                 grad = grad + jac_ref[i * 8 + b, :, lanes].astype(F32) * vec[b : b + 1]
             return grad
 
-        terms[:, lanes] = lax.fori_loop(0, rows // 8, blocks, jnp.zeros((CPAR, 128), F32))
+        terms[:, lanes] = lax.fori_loop(0, rows // 8, blocks, jnp.zeros((CPAR, 128), F32), unroll=4)
     top, rest = halves(terms[...])
     blank = jnp.zeros_like(top)
     both = jnp.concatenate([top, blank, rest, blank], axis=0)
@@ -259,7 +247,7 @@
         compiler_params=LIMIT,
         name="source_step",
     )(block_count, obs, wt, js, ap, seg)
-    live, near_ap, near_seg, near_jac, code = pl.pallas_call(
+    live, near_ap, near_seg, near_jac, code, early = pl.pallas_call(
         near_kernel,
         out_shape=(
             plane,
@@ -267,29 +255,21 @@
             pltpu.VMEM((OBS, slots), jnp.int32),
             pltpu.VMEM((OBS, CPAR, slots), BF16),
             pltpu.VMEM((2 * SLOTS, slots), F32),
+            rows,
         ),
-        in_specs=[SMEM, VMEM] + [HBM] * 4,
-        out_specs=(VMEM,) * 5,
-        scratch_shapes=[pltpu.SemaphoreType.DMA((4,))],
+        in_specs=[SMEM] + [HBM] * 5,
+        out_specs=(VMEM,) * 6,
+        scratch_shapes=[pltpu.VMEM((1, slots), jnp.int32), pltpu.VMEM((CPAR, slots), F32), pltpu.SemaphoreType.DMA((8,))],
         compiler_params=LIMIT,
         name="near_step",
-    )(block_count, cal_index[None, :], wt, ap, seg, jac)
-    early = pl.pallas_call(
-        early_kernel,
-        out_shape=rows,
-        in_specs=[VMEM] * 3,
-        out_specs=VMEM,
-        scratch_shapes=[pltpu.VMEM((CPAR, slots), F32)],
-        compiler_params=LIMIT,
-        name="early_step",
-    )(live, near_jac, code)
+    )(block_count, far(cal_index[None, :]), wt, ap, seg, jac)
     total = sums + moved(sums, 1, 0, 0, 0)
     total = (total + moved(total, 0, 1, 0, 0)) + (moved(total, 0, 2, 0, 0) + moved(total, 0, 3, 0, 0))
     total = (total + moved(total, 0, 0, 1, 0)) + (moved(total, 0, 0, 2, 0) + moved(total, 0, 0, 3, 0))
     total = total + moved(total, 0, 0, 0, 1)
+    total, code = lax.optimization_barrier((total, code))
     total = total + moved(total, 0, 0, 0, 2)
     total = total + moved(total, 0, 0, 0, 6)
-    place = lax.axis_index("mem").astype(jnp.int32)[None]
     att_out, new_resid, send = pl.pallas_call(
         residual_kernel,
         out_shape=(
@@ -297,12 +277,12 @@
             jax.ShapeDtypeStruct((OBS, slots), F32),
             rows,
         ),
-        in_specs=[SMEM] + [VMEM] * 8,
+        in_specs=[VMEM] * 8,
         out_specs=(VMEM,) * 3,
         scratch_shapes=[pltpu.VMEM((OBS, slots), F32), pltpu.VMEM((CPAR, slots), F32)],
         compiler_params=LIMIT,
         name="residual_step",
-    )(place, total, live, near_ap, near_seg, near_jac, resid_one, code, early)
+    )(total, live, near_ap, near_seg, near_jac, resid_one, code, early)
     got = lax.all_to_all(send.reshape(devices, 1, -1), AXES, 0, 0, tiled=True)
     cal_update = pl.pallas_call(
         gather_kernel,

time: 83.3 us -> 79 us (0.948)
  Pallas kernels: 15.9 us -> 10.8 us
  blocking collectives: 36.3 us -> 38.4 us
    pallas_call x1, Pallas kernels: 7.14 us -> 3.86 us  [body(): pl.pallas_call(source_kernel, out_shape=(pltpu.VMEM((64, 128), F32), jax....]
    all_to_all x1, blocking collectives: 36.3 us -> 38.4 us  [body(): got = lax.all_to_all(send.reshape(devices, 1, -1), AXES, 0, 0, tiled=True)]
    pallas_call x1 -> x0, Pallas kernels: 1.73 us -> none  [body(): pl.pallas_call(early_kernel, out_shape=rows, in_specs=[VMEM] * 3, out_spe...]
  transfers between devices with their start and end apart: 10 -> 10, of which waited for: 8 -> 8; matrix products, arithmetic and copies ran while one was open for 0% -> 0% of each run, Pallas kernels for 5% -> 4%
where the time goes in v3:
time: 79 us; the launch traced here: 78.8 us
  blocking collectives  38.4 us (49%)
  starting transfers between devices  19.1 us (24%)
  Pallas kernels  10.8 us (14%)
  waiting for transfers between devices  9.08 us (11%)
  between operations  1.33 us (2%)
    all_to_all x1, blocking collectives, body(): got = lax.all_to_all(send.reshape(devices, 1, -1), AXES, 0, 0, tiled=True)  38.4 us
    ppermute x10, starting transfers between devices, moved(): return lax.ppermute(value, AXES, step_pairs(*step))  19.1 us
    ppermute x10, waiting for transfers between devices, moved(): return lax.ppermute(value, AXES, step_pairs(*step))  9.08 us
    pallas_call x1, Pallas kernels, body(): pl.pallas_call(source_kernel, out_shape=(pltpu.VMEM((64, 128), F32), jax....  3.86 us
    pallas_call x1, Pallas kernels, body(): pl.pallas_call(near_kernel, out_shape=(plane, pltpu.VMEM((4, OBS, slots),...  3.11 us
    pallas_call x1, Pallas kernels, body(): pl.pallas_call(residual_kernel, out_shape=(jax.ShapeDtypeStruct((4, KNOTS...  2.74 us
  transfers between devices with their start and end apart: 10, of which 8 were waited for; matrix products, arithmetic and copies ran while one was open for 0% of the time, Pallas kernels for 4%

profile of v3, /device:TPU:1, one launch (start us, length us, event | category | flops | bytes accessed | tf_op | source)
XLA Modules:
  0.0 78.8 jit_solution(454824797239120008)
XLA Ops:
  1.3 3.9 %source_step.1 = (f32[64,128]{1,0:T(8,128)S(1)}, f32[5,512]{1,0:T(8,128)}, f32[64,512]{1,0:T(8,128)S(1)}) custom-call(s32[1]{0:T(128)S(6)} %copy.13.count_ref, f32[64,512]{1,0:T(8,128)} %bitcast.20, f32[64,512]{1,0:T(8,128)} %bitcast.16, f32[5,64,512]{2,1,0:T(8,128)} %bitcast.15, f32[4,64,512]{2,1,0:T(8,128)} %bitcast.13, s32[64,512]{1,0:T(8,128)} %bitcast.18), custom_call_target="tpu_custom_call" | custom-call | tf_op jit(solution)/shard_map/source_step/pallas_call | solution.py:233
  5.1 3.3 %collective-permute-start = (f32[64,128]{1,0:T(8,128)S(1)}, f32[64,128]{1,0:T(8,128)S(1)}, u32[]{:S(2)}, u32[]{:S(2)}) collective-permute-start(f32[64,128]{1,0:T(8,128)S(1)} %get-tuple-element.19), channel_id=1, source_target_pairs={{0,1},{1,0},{2,3},{3,2},{4,5},{5,4},{6,7},{7,6},{8,9},{9,8},{10,11... | collective-permute-start | bytes 98312 | tf_op jit(solution)/shard_map/ppermute | solution.py:222
  8.5 0.9 %collective-permute-done = f32[64,128]{1,0:T(8,128)S(1)} collective-permute-done((f32[64,128]{1,0:T(8,128)S(1)}, f32[64,128]{1,0:T(8,128)S(1)}, u32[]{:S(2)}, u32[]{:S(2)}) %collective-permute-start) | collective-permute-done | bytes 32800 | tf_op jit(solution)/shard_map/ppermute | solution.py:222
  9.3 0.7 collective-permute-start.3
  10.1 0.5 collective-permute-start.2
  10.6 2.0 %collective-permute-start.1 = (f32[64,128]{1,0:T(8,128)S(1)}, f32[64,128]{1,0:T(8,128)S(1)}, u32[]{:S(2)}, u32[]{:S(2)}) collective-permute-start(f32[64,128]{1,0:T(8,128)S(1)} %add.30), channel_id=1, source_target_pairs={{0,2},{1,3},{2,0},{3,1},{4,6},{5,7},{6,4},{7,5},{8,10},{9,11},{10,... | collective-permute-start | bytes 98312 | tf_op jit(solution)/shard_map/ppermute | solution.py:222
  12.6 0.7 collective-permute-done.3
  13.3 1.1 %collective-permute-done.2 = f32[64,128]{1,0:T(8,128)S(1)} collective-permute-done((f32[64,128]{1,0:T(8,128)S(1)}, f32[64,128]{1,0:T(8,128)S(1)}, u32[]{:S(2)}, u32[]{:S(2)}) %collective-permute-start.2) | collective-permute-done | bytes 32800 | tf_op jit(solution)/shard_map/ppermute | solution.py:222
  14.5 0.1 collective-permute-done.1
  14.6 2.6 %collective-permute-start.6 = (f32[64,128]{1,0:T(8,128)S(1)}, f32[64,128]{1,0:T(8,128)S(1)}, u32[]{:S(2)}, u32[]{:S(2)}) collective-permute-start(f32[64,128]{1,0:T(8,128)S(1)} %add_add_fusion.1), channel_id=1, source_target_pairs={{0,136},{1,137},{2,138},{3,139},{4,140},{5,141},{6,142},{7,143},{8... | collective-permute-start | bytes 98312 | tf_op jit(solution)/shard_map/ppermute | solution.py:222
  17.2 0.3 collective-permute-start.5
  17.5 0.4 collective-permute-start.4
  17.9 0.7 collective-permute-done.6
  18.6 2.8 %collective-permute-done.5 = f32[64,128]{1,0:T(8,128)S(1)} collective-permute-done((f32[64,128]{1,0:T(8,128)S(1)}, f32[64,128]{1,0:T(8,128)S(1)}, u32[]{:S(2)}, u32[]{:S(2)}) %collective-permute-start.5) | collective-permute-done | bytes 32800 | tf_op jit(solution)/shard_map/ppermute | solution.py:222
  21.5 0.0 collective-permute-done.4
  21.5 1.7 %collective-permute-start.7 = (f32[64,128]{1,0:T(8,128)S(1)}, f32[64,128]{1,0:T(8,128)S(1)}, u32[]{:S(2)}, u32[]{:S(2)}) collective-permute-start(f32[64,128]{1,0:T(8,128)S(1)} %add_add_fusion), channel_id=1, source_target_pairs={{0,16},{1,17},{2,18},{3,19},{4,20},{5,21},{6,22},{7,23},{8,24},{9,... | collective-permute-start | bytes 98312 | tf_op jit(solution)/shard_map/ppermute | solution.py:222
  23.2 3.1 %near_step.1 = (f32[64,512]{1,0:T(8,128)S(1)}, f32[4,64,512]{2,1,0:T(8,128)S(1)}, s32[64,512]{1,0:T(8,128)S(1)}, bf16[64,64,512]{2,1,0:T(8,128)(2,1)S(1)}, f32[8...) custom-call(s32[1]{0:T(128)S(6)} %copy.13.count_ref, s32[1,512]{1,0:T(1,128)} %bitcast.21, f32[64,512]{1,0:T(8,128)} %bitcast.17, ...), custom_call_target="tpu_custom_call" | custom-call | tf_op jit(solution)/shard_map/near_step/pallas_call | solution.py:250
  26.3 0.0 collective-permute-done.7
  26.3 3.1 %collective-permute-start.8 = (f32[64,128]{1,0:T(8,128)S(1)}, f32[64,128]{1,0:T(8,128)S(1)}, u32[]{:S(2)}, u32[]{:S(2)}) collective-permute-start(f32[64,128]{1,0:T(8,128)S(1)} %add.37), channel_id=1, source_target_pairs={{0,32},{1,33},{2,34},{3,35},{4,36},{5,37},{6,38},{7,39},{8,40},{9,... | collective-permute-start | bytes 98312 | tf_op jit(solution)/shard_map/ppermute | solution.py:222
  29.4 1.4 %collective-permute-done.8 = f32[64,128]{1,0:T(8,128)S(1)} collective-permute-done((f32[64,128]{1,0:T(8,128)S(1)}, f32[64,128]{1,0:T(8,128)S(1)}, u32[]{:S(2)}, u32[]{:S(2)}) %collective-permute-start.8) | collective-permute-done | bytes 32800 | tf_op jit(solution)/shard_map/ppermute | solution.py:222
  30.8 4.4 %collective-permute-start.9 = (f32[64,128]{1,0:T(8,128)S(1)}, f32[64,128]{1,0:T(8,128)S(1)}, u32[]{:S(2)}, u32[]{:S(2)}) collective-permute-start(f32[64,128]{1,0:T(8,128)S(1)} %add.38), channel_id=1, source_target_pairs={{0,96},{1,97},{2,98},{3,99},{4,100},{5,101},{6,102},{7,103},{8,104... | collective-permute-start | bytes 98312 | tf_op jit(solution)/shard_map/ppermute | solution.py:222
  35.2 1.3 %collective-permute-done.9 = f32[64,128]{1,0:T(8,128)S(1)} collective-permute-done((f32[64,128]{1,0:T(8,128)S(1)}, f32[64,128]{1,0:T(8,128)S(1)}, u32[]{:S(2)}, u32[]{:S(2)}) %collective-permute-start.9) | collective-permute-done | bytes 32800 | tf_op jit(solution)/shard_map/ppermute | solution.py:222
  36.5 2.7 %residual_step.1 = (f32[4,64]{1,0:T(4,128)}, f32[64,512]{1,0:T(8,128)}, f32[1280,128]{1,0:T(8,128)S(1)}) custom-call(f32[64,128]{1,0:T(8,128)S(1)} %add.39.sums_ref, f32[64,512]{1,0:T(8,128)S(1)} %get-tuple-element.22.live_ref, f32[4,64,512]{2,1,0:T(8,128)S(1)} %get-tuple-element.23.ap_ref, s32[64,512]{1,0:T(8,128)S(1)} %get-tuple-element.24.seg_ref, ...), custom_call_target="tpu_custom_call" | custom-call | tf_op jit(solution)/shard_map/residual_step/pallas_call | solution.py:273
  39.3 38.4 %all_to_all.5 = f32[256,1,640]{2,1,0:T(1,128)S(1)} all-to-all(f32[256,1,640]{2,1,0:T(1,128)S(1)} %bitcast.11), channel_id=1, replica_groups=mesh['grp'=16,'mem'=16] {'grp','mem'}, dimensions={0} | all-to-all | bytes 1310720 | tf_op jit(solution)/shard_map/all_to_all | solution.py:286
  77.7 1.1 %calibration_step.1 = f32[64,64]{1,0:T(8,128)} custom-call(f32[1280,128]{1,0:T(8,128)S(1)} %bitcast.10), custom_call_target="tpu_custom_call" | custom-call | tf_op jit(solution)/shard_map/calibration_step/pallas_call | solution.py:287
  (6 shorter events, 0.0 us)
Async XLA Ops:
  5.1 4.2 %collective-permute-start = (f32[64,128]{1,0:T(8,128)S(1)}, f32[64,128]{1,0:T(8,128)S(1)}, u32[]{:S(2)}, u32[]{:S(2)}) collective-permute-start(f32[64,128]{1,0:T(8,128)S(1)} %get-tuple-element.19), channel_id=1, source_target_pairs={{0,1},{1,0},{2,3},{3,2},{4,5},{5,4},{6,7},{7,6},{8,9},{9,8},{10,11... | collective-permute-start | bytes 98312 | tf_op jit(solution)/shard_map/ppermute | solution.py:222
  9.3 4.0 %collective-permute-start.3 = (f32[64,128]{1,0:T(8,128)S(1)}, f32[64,128]{1,0:T(8,128)S(1)}, u32[]{:S(2)}, u32[]{:S(2)}) collective-permute-start(f32[64,128]{1,0:T(8,128)S(1)} %add.30), channel_id=1, source_target_pairs={{0,6},{1,7},{2,4},{3,5},{4,2},{5,3},{6,0},{7,1},{8,14},{9,15},{10,... | collective-permute-start | bytes 98312 | tf_op jit(solution)/shard_map/ppermute | solution.py:222
  10.1 4.4 %collective-permute-start.2 = (f32[64,128]{1,0:T(8,128)S(1)}, f32[64,128]{1,0:T(8,128)S(1)}, u32[]{:S(2)}, u32[]{:S(2)}) collective-permute-start(f32[64,128]{1,0:T(8,128)S(1)} %add.30), channel_id=1, source_target_pairs={{0,4},{1,5},{2,6},{3,7},{4,0},{5,1},{6,2},{7,3},{8,12},{9,13},{10,... | collective-permute-start | bytes 98312 | tf_op jit(solution)/shard_map/ppermute | solution.py:222
  10.6 3.9 %collective-permute-start.1 = (f32[64,128]{1,0:T(8,128)S(1)}, f32[64,128]{1,0:T(8,128)S(1)}, u32[]{:S(2)}, u32[]{:S(2)}) collective-permute-start(f32[64,128]{1,0:T(8,128)S(1)} %add.30), channel_id=1, source_target_pairs={{0,2},{1,3},{2,0},{3,1},{4,6},{5,7},{6,4},{7,5},{8,10},{9,11},{10,... | collective-permute-start | bytes 98312 | tf_op jit(solution)/shard_map/ppermute | solution.py:222
  14.6 4.1 %collective-permute-start.6 = (f32[64,128]{1,0:T(8,128)S(1)}, f32[64,128]{1,0:T(8,128)S(1)}, u32[]{:S(2)}, u32[]{:S(2)}) collective-permute-start(f32[64,128]{1,0:T(8,128)S(1)} %add_add_fusion.1), channel_id=1, source_target_pairs={{0,136},{1,137},{2,138},{3,139},{4,140},{5,141},{6,142},{7,143},{8... | collective-permute-start | bytes 98312 | tf_op jit(solution)/shard_map/ppermute | solution.py:222
  17.2 4.3 %collective-permute-start.5 = (f32[64,128]{1,0:T(8,128)S(1)}, f32[64,128]{1,0:T(8,128)S(1)}, u32[]{:S(2)}, u32[]{:S(2)}) collective-permute-start(f32[64,128]{1,0:T(8,128)S(1)} %add_add_fusion.1), channel_id=1, source_target_pairs={{0,8},{1,9},{2,10},{3,11},{4,12},{5,13},{6,14},{7,15},{8,0},{9,1},... | collective-permute-start | bytes 98312 | tf_op jit(solution)/shard_map/ppermute | solution.py:222
  17.5 3.9 %collective-permute-start.4 = (f32[64,128]{1,0:T(8,128)S(1)}, f32[64,128]{1,0:T(8,128)S(1)}, u32[]{:S(2)}, u32[]{:S(2)}) collective-permute-start(f32[64,128]{1,0:T(8,128)S(1)} %add_add_fusion.1), channel_id=1, source_target_pairs={{0,128},{1,129},{2,130},{3,131},{4,132},{5,133},{6,134},{7,135},{8... | collective-permute-start | bytes 98312 | tf_op jit(solution)/shard_map/ppermute | solution.py:222
  21.5 4.8 %collective-permute-start.7 = (f32[64,128]{1,0:T(8,128)S(1)}, f32[64,128]{1,0:T(8,128)S(1)}, u32[]{:S(2)}, u32[]{:S(2)}) collective-permute-start(f32[64,128]{1,0:T(8,128)S(1)} %add_add_fusion), channel_id=1, source_target_pairs={{0,16},{1,17},{2,18},{3,19},{4,20},{5,21},{6,22},{7,23},{8,24},{9,... | collective-permute-start | bytes 98312 | tf_op jit(solution)/shard_map/ppermute | solution.py:222
  26.3 4.5 %collective-permute-start.8 = (f32[64,128]{1,0:T(8,128)S(1)}, f32[64,128]{1,0:T(8,128)S(1)}, u32[]{:S(2)}, u32[]{:S(2)}) collective-permute-start(f32[64,128]{1,0:T(8,128)S(1)} %add.37), channel_id=1, source_target_pairs={{0,32},{1,33},{2,34},{3,35},{4,36},{5,37},{6,38},{7,39},{8,40},{9,... | collective-permute-start | bytes 98312 | tf_op jit(solution)/shard_map/ppermute | solution.py:222
  30.8 5.7 %collective-permute-start.9 = (f32[64,128]{1,0:T(8,128)S(1)}, f32[64,128]{1,0:T(8,128)S(1)}, u32[]{:S(2)}, u32[]{:S(2)}) collective-permute-start(f32[64,128]{1,0:T(8,128)S(1)} %add.38), channel_id=1, source_target_pairs={{0,96},{1,97},{2,98},{3,99},{4,100},{5,101},{6,102},{7,103},{8,104... | collective-permute-start | bytes 98312 | tf_op jit(solution)/shard_map/ppermute | solution.py:222

commit v4 on v3

--- a/solution.py
+++ b/solution.py
@@ -263,13 +263,12 @@
         compiler_params=LIMIT,
         name="near_step",
     )(block_count, far(cal_index[None, :]), wt, ap, seg, jac)
-    total = sums + moved(sums, 1, 0, 0, 0)
+    total = sums
     total = (total + moved(total, 0, 1, 0, 0)) + (moved(total, 0, 2, 0, 0) + moved(total, 0, 3, 0, 0))
     total = (total + moved(total, 0, 0, 1, 0)) + (moved(total, 0, 0, 2, 0) + moved(total, 0, 0, 3, 0))
-    total = total + moved(total, 0, 0, 0, 1)
+    total = (total + moved(total, 0, 0, 0, 1)) + (moved(total, 0, 0, 0, 6) + moved(total, 0, 0, 0, 7))
     total, code = lax.optimization_barrier((total, code))
-    total = total + moved(total, 0, 0, 0, 2)
-    total = total + moved(total, 0, 0, 0, 6)
+    total = (total + moved(total, 1, 0, 0, 0)) + (moved(total, 0, 0, 0, 2) + moved(total, 1, 0, 0, 2))
     att_out, new_resid, send = pl.pallas_call(
         residual_kernel,
         out_shape=(

time: 79 us -> 77 us (0.975)
  blocking collectives: 38.4 us -> 31.5 us
  starting transfers between devices: 19.1 us -> 22.3 us
  waiting for transfers between devices: 9.08 us -> 10.8 us
    all_to_all x1, blocking collectives: 38.4 us -> 31.5 us  [body(): got = lax.all_to_all(send.reshape(devices, 1, -1), AXES, 0, 0, tiled=True)]
    ppermute x10 -> x12, starting transfers between devices: 19.1 us -> 22.3 us  [moved(): return lax.ppermute(value, AXES, step_pairs(*step))]
    ppermute x10 -> x12, waiting for transfers between devices: 9.08 us -> 10.8 us  [moved(): return lax.ppermute(value, AXES, step_pairs(*step))]
  transfers between devices with their start and end apart: 10 -> 12, of which waited for: 8 -> 7; matrix products, arithmetic and copies ran while one was open for 0% -> 0% of each run, Pallas kernels for 4% -> 4%
where the time goes in v4:
time: 77 us; the launch traced here: 76.9 us
  blocking collectives  31.5 us (41%)
  starting transfers between devices  22.3 us (29%)
  Pallas kernels  10.8 us (14%)
  waiting for transfers between devices  10.8 us (14%)
  between operations  1.33 us (2%)
    all_to_all x1, blocking collectives, body(): got = lax.all_to_all(send.reshape(devices, 1, -1), AXES, 0, 0, tiled=True)  31.5 us
    ppermute x12, starting transfers between devices, moved(): return lax.ppermute(value, AXES, step_pairs(*step))  22.3 us
    ppermute x12, waiting for transfers between devices, moved(): return lax.ppermute(value, AXES, step_pairs(*step))  10.8 us
    pallas_call x1, Pallas kernels, body(): pl.pallas_call(source_kernel, out_shape=(pltpu.VMEM((64, 128), F32), jax....  3.86 us
    pallas_call x1, Pallas kernels, body(): pl.pallas_call(near_kernel, out_shape=(plane, pltpu.VMEM((4, OBS, slots),...  3.11 us
    pallas_call x1, Pallas kernels, body(): pl.pallas_call(residual_kernel, out_shape=(jax.ShapeDtypeStruct((4, KNOTS...  2.75 us
  transfers between devices with their start and end apart: 12, of which 7 were waited for; matrix products, arithmetic and copies ran while one was open for 0% of the time, Pallas kernels for 4%

profile of v4, /device:TPU:1, one launch (start us, length us, event | category | flops | bytes accessed | tf_op | source)
XLA Modules:
  0.0 76.9 jit_solution(3870315186922611026)
XLA Ops:
  1.3 3.9 %source_step.1 = (f32[64,128]{1,0:T(8,128)S(1)}, f32[5,512]{1,0:T(8,128)}, f32[64,512]{1,0:T(8,128)S(1)}) custom-call(s32[1]{0:T(128)S(6)} %copy.13.count_ref, f32[64,512]{1,0:T(8,128)} %bitcast.20, f32[64,512]{1,0:T(8,128)} %bitcast.16, f32[5,64,512]{2,1,0:T(8,128)} %bitcast.15, f32[4,64,512]{2,1,0:T(8,128)} %bitcast.13, s32[64,512]{1,0:T(8,128)} %bitcast.18), custom_call_target="tpu_custom_call" | custom-call | tf_op jit(solution)/shard_map/source_step/pallas_call | solution.py:233
  5.1 3.4 %collective-permute-start.2 = (f32[64,128]{1,0:T(8,128)S(1)}, f32[64,128]{1,0:T(8,128)S(1)}, u32[]{:S(2)}, u32[]{:S(2)}) collective-permute-start(f32[64,128]{1,0:T(8,128)S(1)} %get-tuple-element.19), channel_id=1, source_target_pairs={{0,6},{1,7},{2,4},{3,5},{4,2},{5,3},{6,0},{7,1},{8,14},{9,15},{10,... | collective-permute-start | bytes 98312 | tf_op jit(solution)/shard_map/ppermute | solution.py:222
  8.5 0.5 collective-permute-start.1
  9.1 0.2 collective-permute-start
  9.2 0.6 collective-permute-done.2
  9.8 3.0 %collective-permute-done.1 = f32[64,128]{1,0:T(8,128)S(1)} collective-permute-done((f32[64,128]{1,0:T(8,128)S(1)}, f32[64,128]{1,0:T(8,128)S(1)}, u32[]{:S(2)}, u32[]{:S(2)}) %collective-permute-start.1) | collective-permute-done | bytes 32800 | tf_op jit(solution)/shard_map/ppermute | solution.py:222
  12.8 0.0 collective-permute-done
  12.8 2.8 %collective-permute-start.5 = (f32[64,128]{1,0:T(8,128)S(1)}, f32[64,128]{1,0:T(8,128)S(1)}, u32[]{:S(2)}, u32[]{:S(2)}) collective-permute-start(f32[64,128]{1,0:T(8,128)S(1)} %add_add_fusion.3), channel_id=1, source_target_pairs={{0,136},{1,137},{2,138},{3,139},{4,140},{5,141},{6,142},{7,143},{8... | collective-permute-start | bytes 98312 | tf_op jit(solution)/shard_map/ppermute | solution.py:222
  15.6 0.3 collective-permute-start.4
  16.0 0.3 collective-permute-start.3
  16.3 0.6 collective-permute-done.5
  17.0 3.0 %collective-permute-done.4 = f32[64,128]{1,0:T(8,128)S(1)} collective-permute-done((f32[64,128]{1,0:T(8,128)S(1)}, f32[64,128]{1,0:T(8,128)S(1)}, u32[]{:S(2)}, u32[]{:S(2)}) %collective-permute-start.4) | collective-permute-done | bytes 32800 | tf_op jit(solution)/shard_map/ppermute | solution.py:222
  19.9 0.0 collective-permute-done.3
  19.9 5.7 %collective-permute-start.8 = (f32[64,128]{1,0:T(8,128)S(1)}, f32[64,128]{1,0:T(8,128)S(1)}, u32[]{:S(2)}, u32[]{:S(2)}) collective-permute-start(f32[64,128]{1,0:T(8,128)S(1)} %add_add_fusion.2), channel_id=1, source_target_pairs={{0,112},{1,113},{2,114},{3,115},{4,116},{5,117},{6,118},{7,119},{8... | collective-permute-start | bytes 98312 | tf_op jit(solution)/shard_map/ppermute | solution.py:222
  25.6 0.5 collective-permute-start.7
  26.1 1.1 %collective-permute-start.6 = (f32[64,128]{1,0:T(8,128)S(1)}, f32[64,128]{1,0:T(8,128)S(1)}, u32[]{:S(2)}, u32[]{:S(2)}) collective-permute-start(f32[64,128]{1,0:T(8,128)S(1)} %add_add_fusion.2), channel_id=1, source_target_pairs={{0,16},{1,17},{2,18},{3,19},{4,20},{5,21},{6,22},{7,23},{8,24},{9,... | collective-permute-start | bytes 98312 | tf_op jit(solution)/shard_map/ppermute | solution.py:222
  27.2 3.1 %near_step.1 = (f32[64,512]{1,0:T(8,128)S(1)}, f32[4,64,512]{2,1,0:T(8,128)S(1)}, s32[64,512]{1,0:T(8,128)S(1)}, bf16[64,64,512]{2,1,0:T(8,128)(2,1)S(1)}, f32[8...) custom-call(s32[1]{0:T(128)S(6)} %copy.13.count_ref, s32[1,512]{1,0:T(1,128)} %bitcast.21, f32[64,512]{1,0:T(8,128)} %bitcast.17, ...), custom_call_target="tpu_custom_call" | custom-call | tf_op jit(solution)/shard_map/near_step/pallas_call | solution.py:250
  30.3 0.0 collective-permute-done.8
  30.4 0.1 collective-permute-done.7
  30.5 0.0 collective-permute-done.6
  30.5 7.0 %collective-permute-start.11 = (f32[64,128]{1,0:T(8,128)S(1)}, f32[64,128]{1,0:T(8,128)S(1)}, u32[]{:S(2)}, u32[]{:S(2)}) collective-permute-start(f32[64,128]{1,0:T(8,128)S(1)} %add_add_fusion.1), channel_id=1, source_target_pairs={{0,33},{1,32},{2,35},{3,34},{4,37},{5,36},{6,39},{7,38},{8,41},{9,... | collective-permute-start | bytes 98312 | tf_op jit(solution)/shard_map/ppermute | solution.py:222
  37.5 0.3 collective-permute-start.10
  37.8 0.2 collective-permute-start.9
  38.0 1.7 %collective-permute-done.11 = f32[64,128]{1,0:T(8,128)S(1)} collective-permute-done((f32[64,128]{1,0:T(8,128)S(1)}, f32[64,128]{1,0:T(8,128)S(1)}, u32[]{:S(2)}, u32[]{:S(2)}) %collective-permute-start.11) | collective-permute-done | bytes 32800 | tf_op jit(solution)/shard_map/ppermute | solution.py:222
  39.7 1.8 %collective-permute-done.10 = f32[64,128]{1,0:T(8,128)S(1)} collective-permute-done((f32[64,128]{1,0:T(8,128)S(1)}, f32[64,128]{1,0:T(8,128)S(1)}, u32[]{:S(2)}, u32[]{:S(2)}) %collective-permute-start.10) | collective-permute-done | bytes 32800 | tf_op jit(solution)/shard_map/ppermute | solution.py:222
  41.5 0.0 collective-permute-done.9
  41.5 2.7 %residual_step.1 = (f32[4,64]{1,0:T(4,128)}, f32[64,512]{1,0:T(8,128)}, f32[1280,128]{1,0:T(8,128)S(1)}) custom-call(f32[64,128]{1,0:T(8,128)S(1)} %add_add_fusion.sums_ref, f32[64,512]{1,0:T(8,128)S(1)} %get-tuple-element.22.live_ref, f32[4,64,512]{2,1,0:T(8,128)S(1)} %get-tuple-element.23.ap_ref, s32[64,512]{1,0:T(8,128)S(1)} %get-tuple-element.24.seg_ref, ...), custom_call_target="tpu_custom_call" | custom-call | tf_op jit(solution)/shard_map/residual_step/pallas_call | solution.py:272
  44.3 31.5 %all_to_all.5 = f32[256,1,640]{2,1,0:T(1,128)S(1)} all-to-all(f32[256,1,640]{2,1,0:T(1,128)S(1)} %bitcast.11), channel_id=1, replica_groups=mesh['grp'=16,'mem'=16] {'grp','mem'}, dimensions={0} | all-to-all | bytes 1310720 | tf_op jit(solution)/shard_map/all_to_all | solution.py:285
  75.8 1.1 %calibration_step.1 = f32[64,64]{1,0:T(8,128)} custom-call(f32[1280,128]{1,0:T(8,128)S(1)} %bitcast.10), custom_call_target="tpu_custom_call" | custom-call | tf_op jit(solution)/shard_map/calibration_step/pallas_call | solution.py:286
  (4 shorter events, 0.0 us)
Async XLA Ops:
  5.1 4.7 %collective-permute-start.2 = (f32[64,128]{1,0:T(8,128)S(1)}, f32[64,128]{1,0:T(8,128)S(1)}, u32[]{:S(2)}, u32[]{:S(2)}) collective-permute-start(f32[64,128]{1,0:T(8,128)S(1)} %get-tuple-element.19), channel_id=1, source_target_pairs={{0,6},{1,7},{2,4},{3,5},{4,2},{5,3},{6,0},{7,1},{8,14},{9,15},{10,... | collective-permute-start | bytes 98312 | tf_op jit(solution)/shard_map/ppermute | solution.py:222
  8.5 4.3 %collective-permute-start.1 = (f32[64,128]{1,0:T(8,128)S(1)}, f32[64,128]{1,0:T(8,128)S(1)}, u32[]{:S(2)}, u32[]{:S(2)}) collective-permute-start(f32[64,128]{1,0:T(8,128)S(1)} %get-tuple-element.19), channel_id=1, source_target_pairs={{0,4},{1,5},{2,6},{3,7},{4,0},{5,1},{6,2},{7,3},{8,12},{9,13},{10,... | collective-permute-start | bytes 98312 | tf_op jit(solution)/shard_map/ppermute | solution.py:222
  9.1 3.8 %collective-permute-start = (f32[64,128]{1,0:T(8,128)S(1)}, f32[64,128]{1,0:T(8,128)S(1)}, u32[]{:S(2)}, u32[]{:S(2)}) collective-permute-start(f32[64,128]{1,0:T(8,128)S(1)} %get-tuple-element.19), channel_id=1, source_target_pairs={{0,2},{1,3},{2,0},{3,1},{4,6},{5,7},{6,4},{7,5},{8,10},{9,11},{10,... | collective-permute-start | bytes 98312 | tf_op jit(solution)/shard_map/ppermute | solution.py:222
  12.8 4.1 %collective-permute-start.5 = (f32[64,128]{1,0:T(8,128)S(1)}, f32[64,128]{1,0:T(8,128)S(1)}, u32[]{:S(2)}, u32[]{:S(2)}) collective-permute-start(f32[64,128]{1,0:T(8,128)S(1)} %add_add_fusion.3), channel_id=1, source_target_pairs={{0,136},{1,137},{2,138},{3,139},{4,140},{5,141},{6,142},{7,143},{8... | collective-permute-start | bytes 98312 | tf_op jit(solution)/shard_map/ppermute | solution.py:222
  15.6 4.3 %collective-permute-start.4 = (f32[64,128]{1,0:T(8,128)S(1)}, f32[64,128]{1,0:T(8,128)S(1)}, u32[]{:S(2)}, u32[]{:S(2)}) collective-permute-start(f32[64,128]{1,0:T(8,128)S(1)} %add_add_fusion.3), channel_id=1, source_target_pairs={{0,8},{1,9},{2,10},{3,11},{4,12},{5,13},{6,14},{7,15},{8,0},{9,1},... | collective-permute-start | bytes 98312 | tf_op jit(solution)/shard_map/ppermute | solution.py:222
  16.0 3.9 %collective-permute-start.3 = (f32[64,128]{1,0:T(8,128)S(1)}, f32[64,128]{1,0:T(8,128)S(1)}, u32[]{:S(2)}, u32[]{:S(2)}) collective-permute-start(f32[64,128]{1,0:T(8,128)S(1)} %add_add_fusion.3), channel_id=1, source_target_pairs={{0,128},{1,129},{2,130},{3,131},{4,132},{5,133},{6,134},{7,135},{8... | collective-permute-start | bytes 98312 | tf_op jit(solution)/shard_map/ppermute | solution.py:222
  19.9 10.4 %collective-permute-start.8 = (f32[64,128]{1,0:T(8,128)S(1)}, f32[64,128]{1,0:T(8,128)S(1)}, u32[]{:S(2)}, u32[]{:S(2)}) collective-permute-start(f32[64,128]{1,0:T(8,128)S(1)} %add_add_fusion.2), channel_id=1, source_target_pairs={{0,112},{1,113},{2,114},{3,115},{4,116},{5,117},{6,118},{7,119},{8... | collective-permute-start | bytes 98312 | tf_op jit(solution)/shard_map/ppermute | solution.py:222
  25.6 4.9 %collective-permute-start.7 = (f32[64,128]{1,0:T(8,128)S(1)}, f32[64,128]{1,0:T(8,128)S(1)}, u32[]{:S(2)}, u32[]{:S(2)}) collective-permute-start(f32[64,128]{1,0:T(8,128)S(1)} %add_add_fusion.2), channel_id=1, source_target_pairs={{0,96},{1,97},{2,98},{3,99},{4,100},{5,101},{6,102},{7,103},{8,104... | collective-permute-start | bytes 98312 | tf_op jit(solution)/shard_map/ppermute | solution.py:222
  26.1 4.3 %collective-permute-start.6 = (f32[64,128]{1,0:T(8,128)S(1)}, f32[64,128]{1,0:T(8,128)S(1)}, u32[]{:S(2)}, u32[]{:S(2)}) collective-permute-start(f32[64,128]{1,0:T(8,128)S(1)} %add_add_fusion.2), channel_id=1, source_target_pairs={{0,16},{1,17},{2,18},{3,19},{4,20},{5,21},{6,22},{7,23},{8,24},{9,... | collective-permute-start | bytes 98312 | tf_op jit(solution)/shard_map/ppermute | solution.py:222
  30.5 9.2 %collective-permute-start.11 = (f32[64,128]{1,0:T(8,128)S(1)}, f32[64,128]{1,0:T(8,128)S(1)}, u32[]{:S(2)}, u32[]{:S(2)}) collective-permute-start(f32[64,128]{1,0:T(8,128)S(1)} %add_add_fusion.1), channel_id=1, source_target_pairs={{0,33},{1,32},{2,35},{3,34},{4,37},{5,36},{6,39},{7,38},{8,41},{9,... | collective-permute-start | bytes 98312 | tf_op jit(solution)/shard_map/ppermute | solution.py:222
  37.5 4.0 %collective-permute-start.10 = (f32[64,128]{1,0:T(8,128)S(1)}, f32[64,128]{1,0:T(8,128)S(1)}, u32[]{:S(2)}, u32[]{:S(2)}) collective-permute-start(f32[64,128]{1,0:T(8,128)S(1)} %add_add_fusion.1), channel_id=1, source_target_pairs={{0,32},{1,33},{2,34},{3,35},{4,36},{5,37},{6,38},{7,39},{8,40},{9,... | collective-permute-start | bytes 98312 | tf_op jit(solution)/shard_map/ppermute | solution.py:222
  37.8 3.7 %collective-permute-start.9 = (f32[64,128]{1,0:T(8,128)S(1)}, f32[64,128]{1,0:T(8,128)S(1)}, u32[]{:S(2)}, u32[]{:S(2)}) collective-permute-start(f32[64,128]{1,0:T(8,128)S(1)} %add_add_fusion.1), channel_id=1, source_target_pairs={{0,1},{1,0},{2,3},{3,2},{4,5},{5,4},{6,7},{7,6},{8,9},{9,8},{10,11... | collective-permute-start | bytes 98312 | tf_op jit(solution)/shard_map/ppermute | solution.py:222

commit v5 on v4

--- a/solution.py
+++ b/solution.py
@@ -176,13 +176,10 @@
     for c in range(slots // 128):
         lanes = slice(128 * c, 128 * c + 128)
 
-        def blocks(i, grad):
-            vec = vec_buf[pl.ds(pl.multiple_of(i * 8, 8), 8), lanes]
-            for b in range(8):
-                grad = grad + jac_ref[i * 8 + b, :, lanes].astype(F32) * vec[b : b + 1]
-            return grad
-
-        terms[:, lanes] = lax.fori_loop(0, rows // 8, blocks, jnp.zeros((CPAR, 128), F32), unroll=4)
+        grad = jnp.zeros((CPAR, 128), F32)
+        for r in range(rows):
+            grad = grad + jac_ref[r, :, lanes].astype(F32) * vec_buf[r : r + 1, lanes]
+        terms[:, lanes] = grad
     top, rest = halves(terms[...])
     blank = jnp.zeros_like(top)
     both = jnp.concatenate([top, blank, rest, blank], axis=0)
@@ -199,11 +196,11 @@
     devices = got_ref.shape[0] // (SLOTS + 1)
     ids = lax.broadcasted_iota(jnp.int32, (devices, 64), 1).astype(F32)
     offsets = got_ref[pl.ds(SLOTS, devices, stride=SLOTS + 1), :]
-    total = jnp.zeros((64, 256), F32)
+    picks, parts = [], []
     for j in range(SLOTS):
-        pick = (ids == offsets[:, j : j + 1]).astype(F32).astype(BF16)
-        top, rest = halves(got_ref[pl.ds(j, devices, stride=SLOTS + 1), :])
-        total = total + lax.dot_general(pick, jnp.concatenate([top, rest], axis=1), TN, preferred_element_type=F32)
+        picks.append((ids == offsets[:, j : j + 1]).astype(F32).astype(BF16))
+        parts.append(jnp.concatenate(halves(got_ref[pl.ds(j, devices, stride=SLOTS + 1), :]), axis=1))
+    total = lax.dot_general(jnp.concatenate(picks, axis=0), jnp.concatenate(parts, axis=0), TN, preferred_element_type=F32)
     sums = total[:, 0:128] + total[:, 128:256]
     out_ref[...] = sums[:, 0:CPAR] / (1.0 + sums[:, CPAR : 2 * CPAR])
 

time: 77 us -> 76.7 us (level)
  no operation moved by 1% of the time
where the time goes in v5:
time: 76.7 us; the launch traced here: 76.6 us
  blocking collectives  31.5 us (41%)
  starting transfers between devices  22.3 us (29%)
  waiting for transfers between devices  10.8 us (14%)
  Pallas kernels  10.6 us (14%)
  between operations  1.33 us (2%)
    all_to_all x1, blocking collectives, body(): got = lax.all_to_all(send.reshape(devices, 1, -1), AXES, 0, 0, tiled=True)  31.5 us
    ppermute x12, starting transfers between devices, moved(): return lax.ppermute(value, AXES, step_pairs(*step))  22.3 us
    ppermute x12, waiting for transfers between devices, moved(): return lax.ppermute(value, AXES, step_pairs(*step))  10.8 us
    pallas_call x1, Pallas kernels, body(): pl.pallas_call(source_kernel, out_shape=(pltpu.VMEM((64, 128), F32), jax....  3.86 us
    pallas_call x1, Pallas kernels, body(): pl.pallas_call(near_kernel, out_shape=(plane, pltpu.VMEM((4, OBS, slots),...  3.11 us
    pallas_call x1, Pallas kernels, body(): pl.pallas_call(residual_kernel, out_shape=(jax.ShapeDtypeStruct((4, KNOTS...  2.47 us
  transfers between devices with their start and end apart: 12, of which 7 were waited for; matrix products, arithmetic and copies ran while one was open for 0% of the time, Pallas kernels for 4%

profile of v5, /device:TPU:1, one launch (start us, length us, event | category | flops | bytes accessed | tf_op | source)
XLA Modules:
  0.0 76.6 jit_solution(2589729966975607594)
XLA Ops:
  1.3 3.9 %source_step.1 = (f32[64,128]{1,0:T(8,128)S(1)}, f32[5,512]{1,0:T(8,128)}, f32[64,512]{1,0:T(8,128)S(1)}) custom-call(s32[1]{0:T(128)S(6)} %copy.13.count_ref, f32[64,512]{1,0:T(8,128)} %bitcast.20, f32[64,512]{1,0:T(8,128)} %bitcast.16, f32[5,64,512]{2,1,0:T(8,128)} %bitcast.15, f32[4,64,512]{2,1,0:T(8,128)} %bitcast.13, s32[64,512]{1,0:T(8,128)} %bitcast.18), custom_call_target="tpu_custom_call" | custom-call | tf_op jit(solution)/shard_map/source_step/pallas_call | solution.py:230
  5.1 3.4 %collective-permute-start.2 = (f32[64,128]{1,0:T(8,128)S(1)}, f32[64,128]{1,0:T(8,128)S(1)}, u32[]{:S(2)}, u32[]{:S(2)}) collective-permute-start(f32[64,128]{1,0:T(8,128)S(1)} %get-tuple-element.19), channel_id=1, source_target_pairs={{0,6},{1,7},{2,4},{3,5},{4,2},{5,3},{6,0},{7,1},{8,14},{9,15},{10,... | collective-permute-start | bytes 98312 | tf_op jit(solution)/shard_map/ppermute | solution.py:219
  8.5 0.5 collective-permute-start.1
  9.1 0.2 collective-permute-start
  9.2 0.6 collective-permute-done.2
  9.8 3.0 %collective-permute-done.1 = f32[64,128]{1,0:T(8,128)S(1)} collective-permute-done((f32[64,128]{1,0:T(8,128)S(1)}, f32[64,128]{1,0:T(8,128)S(1)}, u32[]{:S(2)}, u32[]{:S(2)}) %collective-permute-start.1) | collective-permute-done | bytes 32800 | tf_op jit(solution)/shard_map/ppermute | solution.py:219
  12.8 0.0 collective-permute-done
  12.8 2.8 %collective-permute-start.5 = (f32[64,128]{1,0:T(8,128)S(1)}, f32[64,128]{1,0:T(8,128)S(1)}, u32[]{:S(2)}, u32[]{:S(2)}) collective-permute-start(f32[64,128]{1,0:T(8,128)S(1)} %add_add_fusion.3), channel_id=1, source_target_pairs={{0,136},{1,137},{2,138},{3,139},{4,140},{5,141},{6,142},{7,143},{8... | collective-permute-start | bytes 98312 | tf_op jit(solution)/shard_map/ppermute | solution.py:219
  15.6 0.3 collective-permute-start.4
  16.0 0.3 collective-permute-start.3
  16.3 0.6 collective-permute-done.5
  17.0 3.0 %collective-permute-done.4 = f32[64,128]{1,0:T(8,128)S(1)} collective-permute-done((f32[64,128]{1,0:T(8,128)S(1)}, f32[64,128]{1,0:T(8,128)S(1)}, u32[]{:S(2)}, u32[]{:S(2)}) %collective-permute-start.4) | collective-permute-done | bytes 32800 | tf_op jit(solution)/shard_map/ppermute | solution.py:219
  19.9 0.0 collective-permute-done.3
  19.9 5.7 %collective-permute-start.8 = (f32[64,128]{1,0:T(8,128)S(1)}, f32[64,128]{1,0:T(8,128)S(1)}, u32[]{:S(2)}, u32[]{:S(2)}) collective-permute-start(f32[64,128]{1,0:T(8,128)S(1)} %add_add_fusion.2), channel_id=1, source_target_pairs={{0,112},{1,113},{2,114},{3,115},{4,116},{5,117},{6,118},{7,119},{8... | collective-permute-start | bytes 98312 | tf_op jit(solution)/shard_map/ppermute | solution.py:219
  25.6 0.5 collective-permute-start.7
  26.1 1.1 %collective-permute-start.6 = (f32[64,128]{1,0:T(8,128)S(1)}, f32[64,128]{1,0:T(8,128)S(1)}, u32[]{:S(2)}, u32[]{:S(2)}) collective-permute-start(f32[64,128]{1,0:T(8,128)S(1)} %add_add_fusion.2), channel_id=1, source_target_pairs={{0,16},{1,17},{2,18},{3,19},{4,20},{5,21},{6,22},{7,23},{8,24},{9,... | collective-permute-start | bytes 98312 | tf_op jit(solution)/shard_map/ppermute | solution.py:219
  27.2 3.1 %near_step.1 = (f32[64,512]{1,0:T(8,128)S(1)}, f32[4,64,512]{2,1,0:T(8,128)S(1)}, s32[64,512]{1,0:T(8,128)S(1)}, bf16[64,64,512]{2,1,0:T(8,128)(2,1)S(1)}, f32[8...) custom-call(s32[1]{0:T(128)S(6)} %copy.13.count_ref, s32[1,512]{1,0:T(1,128)} %bitcast.21, f32[64,512]{1,0:T(8,128)} %bitcast.17, ...), custom_call_target="tpu_custom_call" | custom-call | tf_op jit(solution)/shard_map/near_step/pallas_call | solution.py:247
  30.3 0.0 collective-permute-done.8
  30.4 0.1 collective-permute-done.7
  30.5 0.0 collective-permute-done.6
  30.5 7.0 %collective-permute-start.11 = (f32[64,128]{1,0:T(8,128)S(1)}, f32[64,128]{1,0:T(8,128)S(1)}, u32[]{:S(2)}, u32[]{:S(2)}) collective-permute-start(f32[64,128]{1,0:T(8,128)S(1)} %add_add_fusion.1), channel_id=1, source_target_pairs={{0,33},{1,32},{2,35},{3,34},{4,37},{5,36},{6,39},{7,38},{8,41},{9,... | collective-permute-start | bytes 98312 | tf_op jit(solution)/shard_map/ppermute | solution.py:219
  37.5 0.3 collective-permute-start.10
  37.8 0.2 collective-permute-start.9
  38.0 1.7 %collective-permute-done.11 = f32[64,128]{1,0:T(8,128)S(1)} collective-permute-done((f32[64,128]{1,0:T(8,128)S(1)}, f32[64,128]{1,0:T(8,128)S(1)}, u32[]{:S(2)}, u32[]{:S(2)}) %collective-permute-start.11) | collective-permute-done | bytes 32800 | tf_op jit(solution)/shard_map/ppermute | solution.py:219
  39.7 1.8 %collective-permute-done.10 = f32[64,128]{1,0:T(8,128)S(1)} collective-permute-done((f32[64,128]{1,0:T(8,128)S(1)}, f32[64,128]{1,0:T(8,128)S(1)}, u32[]{:S(2)}, u32[]{:S(2)}) %collective-permute-start.10) | collective-permute-done | bytes 32800 | tf_op jit(solution)/shard_map/ppermute | solution.py:219
  41.5 0.0 collective-permute-done.9
  41.5 2.5 %residual_step.1 = (f32[4,64]{1,0:T(4,128)}, f32[64,512]{1,0:T(8,128)}, f32[1280,128]{1,0:T(8,128)S(1)}) custom-call(f32[64,128]{1,0:T(8,128)S(1)} %add_add_fusion.sums_ref, f32[64,512]{1,0:T(8,128)S(1)} %get-tuple-element.22.live_ref, f32[4,64,512]{2,1,0:T(8,128)S(1)} %get-tuple-element.23.ap_ref, s32[64,512]{1,0:T(8,128)S(1)} %get-tuple-element.24.seg_ref, ...), custom_call_target="tpu_custom_call" | custom-call | tf_op jit(solution)/shard_map/residual_step/pallas_call | solution.py:269
  44.0 31.5 %all_to_all.5 = f32[256,1,640]{2,1,0:T(1,128)S(1)} all-to-all(f32[256,1,640]{2,1,0:T(1,128)S(1)} %bitcast.11), channel_id=1, replica_groups=mesh['grp'=16,'mem'=16] {'grp','mem'}, dimensions={0} | all-to-all | bytes 1310720 | tf_op jit(solution)/shard_map/all_to_all | solution.py:282
  75.5 1.1 %calibration_step.1 = f32[64,64]{1,0:T(8,128)} custom-call(f32[1280,128]{1,0:T(8,128)S(1)} %bitcast.10), custom_call_target="tpu_custom_call" | custom-call | tf_op jit(solution)/shard_map/calibration_step/pallas_call | solution.py:283
  (4 shorter events, 0.0 us)
Async XLA Ops:
  5.1 4.7 %collective-permute-start.2 = (f32[64,128]{1,0:T(8,128)S(1)}, f32[64,128]{1,0:T(8,128)S(1)}, u32[]{:S(2)}, u32[]{:S(2)}) collective-permute-start(f32[64,128]{1,0:T(8,128)S(1)} %get-tuple-element.19), channel_id=1, source_target_pairs={{0,6},{1,7},{2,4},{3,5},{4,2},{5,3},{6,0},{7,1},{8,14},{9,15},{10,... | collective-permute-start | bytes 98312 | tf_op jit(solution)/shard_map/ppermute | solution.py:219
  8.5 4.3 %collective-permute-start.1 = (f32[64,128]{1,0:T(8,128)S(1)}, f32[64,128]{1,0:T(8,128)S(1)}, u32[]{:S(2)}, u32[]{:S(2)}) collective-permute-start(f32[64,128]{1,0:T(8,128)S(1)} %get-tuple-element.19), channel_id=1, source_target_pairs={{0,4},{1,5},{2,6},{3,7},{4,0},{5,1},{6,2},{7,3},{8,12},{9,13},{10,... | collective-permute-start | bytes 98312 | tf_op jit(solution)/shard_map/ppermute | solution.py:219
  9.1 3.8 %collective-permute-start = (f32[64,128]{1,0:T(8,128)S(1)}, f32[64,128]{1,0:T(8,128)S(1)}, u32[]{:S(2)}, u32[]{:S(2)}) collective-permute-start(f32[64,128]{1,0:T(8,128)S(1)} %get-tuple-element.19), channel_id=1, source_target_pairs={{0,2},{1,3},{2,0},{3,1},{4,6},{5,7},{6,4},{7,5},{8,10},{9,11},{10,... | collective-permute-start | bytes 98312 | tf_op jit(solution)/shard_map/ppermute | solution.py:219
  12.8 4.1 %collective-permute-start.5 = (f32[64,128]{1,0:T(8,128)S(1)}, f32[64,128]{1,0:T(8,128)S(1)}, u32[]{:S(2)}, u32[]{:S(2)}) collective-permute-start(f32[64,128]{1,0:T(8,128)S(1)} %add_add_fusion.3), channel_id=1, source_target_pairs={{0,136},{1,137},{2,138},{3,139},{4,140},{5,141},{6,142},{7,143},{8... | collective-permute-start | bytes 98312 | tf_op jit(solution)/shard_map/ppermute | solution.py:219
  15.6 4.3 %collective-permute-start.4 = (f32[64,128]{1,0:T(8,128)S(1)}, f32[64,128]{1,0:T(8,128)S(1)}, u32[]{:S(2)}, u32[]{:S(2)}) collective-permute-start(f32[64,128]{1,0:T(8,128)S(1)} %add_add_fusion.3), channel_id=1, source_target_pairs={{0,8},{1,9},{2,10},{3,11},{4,12},{5,13},{6,14},{7,15},{8,0},{9,1},... | collective-permute-start | bytes 98312 | tf_op jit(solution)/shard_map/ppermute | solution.py:219
  16.0 3.9 %collective-permute-start.3 = (f32[64,128]{1,0:T(8,128)S(1)}, f32[64,128]{1,0:T(8,128)S(1)}, u32[]{:S(2)}, u32[]{:S(2)}) collective-permute-start(f32[64,128]{1,0:T(8,128)S(1)} %add_add_fusion.3), channel_id=1, source_target_pairs={{0,128},{1,129},{2,130},{3,131},{4,132},{5,133},{6,134},{7,135},{8... | collective-permute-start | bytes 98312 | tf_op jit(solution)/shard_map/ppermute | solution.py:219
  19.9 10.4 %collective-permute-start.8 = (f32[64,128]{1,0:T(8,128)S(1)}, f32[64,128]{1,0:T(8,128)S(1)}, u32[]{:S(2)}, u32[]{:S(2)}) collective-permute-start(f32[64,128]{1,0:T(8,128)S(1)} %add_add_fusion.2), channel_id=1, source_target_pairs={{0,112},{1,113},{2,114},{3,115},{4,116},{5,117},{6,118},{7,119},{8... | collective-permute-start | bytes 98312 | tf_op jit(solution)/shard_map/ppermute | solution.py:219
  25.6 4.9 %collective-permute-start.7 = (f32[64,128]{1,0:T(8,128)S(1)}, f32[64,128]{1,0:T(8,128)S(1)}, u32[]{:S(2)}, u32[]{:S(2)}) collective-permute-start(f32[64,128]{1,0:T(8,128)S(1)} %add_add_fusion.2), channel_id=1, source_target_pairs={{0,96},{1,97},{2,98},{3,99},{4,100},{5,101},{6,102},{7,103},{8,104... | collective-permute-start | bytes 98312 | tf_op jit(solution)/shard_map/ppermute | solution.py:219
  26.1 4.3 %collective-permute-start.6 = (f32[64,128]{1,0:T(8,128)S(1)}, f32[64,128]{1,0:T(8,128)S(1)}, u32[]{:S(2)}, u32[]{:S(2)}) collective-permute-start(f32[64,128]{1,0:T(8,128)S(1)} %add_add_fusion.2), channel_id=1, source_target_pairs={{0,16},{1,17},{2,18},{3,19},{4,20},{5,21},{6,22},{7,23},{8,24},{9,... | collective-permute-start | bytes 98312 | tf_op jit(solution)/shard_map/ppermute | solution.py:219
  30.5 9.2 %collective-permute-start.11 = (f32[64,128]{1,0:T(8,128)S(1)}, f32[64,128]{1,0:T(8,128)S(1)}, u32[]{:S(2)}, u32[]{:S(2)}) collective-permute-start(f32[64,128]{1,0:T(8,128)S(1)} %add_add_fusion.1), channel_id=1, source_target_pairs={{0,33},{1,32},{2,35},{3,34},{4,37},{5,36},{6,39},{7,38},{8,41},{9,... | collective-permute-start | bytes 98312 | tf_op jit(solution)/shard_map/ppermute | solution.py:219
  37.5 4.0 %collective-permute-start.10 = (f32[64,128]{1,0:T(8,128)S(1)}, f32[64,128]{1,0:T(8,128)S(1)}, u32[]{:S(2)}, u32[]{:S(2)}) collective-permute-start(f32[64,128]{1,0:T(8,128)S(1)} %add_add_fusion.1), channel_id=1, source_target_pairs={{0,32},{1,33},{2,34},{3,35},{4,36},{5,37},{6,38},{7,39},{8,40},{9,... | collective-permute-start | bytes 98312 | tf_op jit(solution)/shard_map/ppermute | solution.py:219
  37.8 3.7 %collective-permute-start.9 = (f32[64,128]{1,0:T(8,128)S(1)}, f32[64,128]{1,0:T(8,128)S(1)}, u32[]{:S(2)}, u32[]{:S(2)}) collective-permute-start(f32[64,128]{1,0:T(8,128)S(1)} %add_add_fusion.1), channel_id=1, source_target_pairs={{0,1},{1,0},{2,3},{3,2},{4,5},{5,4},{6,7},{7,6},{8,9},{9,8},{10,11... | collective-permute-start | bytes 98312 | tf_op jit(solution)/shard_map/ppermute | solution.py:219

commit v6 on v5

--- a/solution.py
+++ b/solution.py
@@ -261,11 +261,11 @@
         name="near_step",
     )(block_count, far(cal_index[None, :]), wt, ap, seg, jac)
     total = sums
+    total = (total + moved(total, 1, 0, 0, 0)) + (moved(total, 0, 0, 0, 1) + moved(total, 1, 0, 0, 1))
     total = (total + moved(total, 0, 1, 0, 0)) + (moved(total, 0, 2, 0, 0) + moved(total, 0, 3, 0, 0))
     total = (total + moved(total, 0, 0, 1, 0)) + (moved(total, 0, 0, 2, 0) + moved(total, 0, 0, 3, 0))
-    total = (total + moved(total, 0, 0, 0, 1)) + (moved(total, 0, 0, 0, 6) + moved(total, 0, 0, 0, 7))
     total, code = lax.optimization_barrier((total, code))
-    total = (total + moved(total, 1, 0, 0, 0)) + (moved(total, 0, 0, 0, 2) + moved(total, 1, 0, 0, 2))
+    total = (total + moved(total, 0, 0, 0, 2)) + (moved(total, 0, 0, 0, 4) + moved(total, 0, 0, 0, 6))
     att_out, new_resid, send = pl.pallas_call(
         residual_kernel,
         out_shape=(

time: 76.7 us -> 76.8 us (level)
  blocking collectives: 31.5 us -> 35.6 us
  starting transfers between devices: 22.3 us -> 18.9 us
    all_to_all x1, blocking collectives: 31.5 us -> 35.6 us  [body(): got = lax.all_to_all(send.reshape(devices, 1, -1), AXES, 0, 0, tiled=True)]
    ppermute x12, starting transfers between devices: 22.3 us -> 18.9 us  [moved(): return lax.ppermute(value, AXES, step_pairs(*step))]
  transfers between devices with their start and end apart: 12 -> 12, of which waited for: 7 -> 5; matrix products, arithmetic and copies ran while one was open for 0% -> 0% of each run, Pallas kernels for 4% -> 4%
where the time goes in v6:
time: 76.8 us; the launch traced here: 76.6 us
  blocking collectives  35.6 us (46%)
  starting transfers between devices  18.9 us (25%)
  Pallas kernels  10.6 us (14%)
  waiting for transfers between devices  10.2 us (13%)
  between operations  1.33 us (2%)
    all_to_all x1, blocking collectives, body(): got = lax.all_to_all(send.reshape(devices, 1, -1), AXES, 0, 0, tiled=True)  35.6 us
    ppermute x12, starting transfers between devices, moved(): return lax.ppermute(value, AXES, step_pairs(*step))  18.9 us
    ppermute x12, waiting for transfers between devices, moved(): return lax.ppermute(value, AXES, step_pairs(*step))  10.2 us
    pallas_call x1, Pallas kernels, body(): pl.pallas_call(source_kernel, out_shape=(pltpu.VMEM((64, 128), F32), jax....  3.86 us
    pallas_call x1, Pallas kernels, body(): pl.pallas_call(near_kernel, out_shape=(plane, pltpu.VMEM((4, OBS, slots),...  3.11 us
    pallas_call x1, Pallas kernels, body(): pl.pallas_call(residual_kernel, out_shape=(jax.ShapeDtypeStruct((4, KNOTS...  2.47 us
  transfers between devices with their start and end apart: 12, of which 5 were waited for; matrix products, arithmetic and copies ran while one was open for 0% of the time, Pallas kernels for 4%

profile of v6, /device:TPU:1, one launch (start us, length us, event | category | flops | bytes accessed | tf_op | source)
XLA Modules:
  0.0 76.6 jit_solution(4494084042253721515)
XLA Ops:
  1.3 3.9 %source_step.1 = (f32[64,128]{1,0:T(8,128)S(1)}, f32[5,512]{1,0:T(8,128)}, f32[64,512]{1,0:T(8,128)S(1)}) custom-call(s32[1]{0:T(128)S(6)} %copy.13.count_ref, f32[64,512]{1,0:T(8,128)} %bitcast.20, f32[64,512]{1,0:T(8,128)} %bitcast.16, f32[5,64,512]{2,1,0:T(8,128)} %bitcast.15, f32[4,64,512]{2,1,0:T(8,128)} %bitcast.13, s32[64,512]{1,0:T(8,128)} %bitcast.18), custom_call_target="tpu_custom_call" | custom-call | tf_op jit(solution)/shard_map/source_step/pallas_call | solution.py:230
  5.1 3.1 %collective-permute-start.2 = (f32[64,128]{1,0:T(8,128)S(1)}, f32[64,128]{1,0:T(8,128)S(1)}, u32[]{:S(2)}, u32[]{:S(2)}) collective-permute-start(f32[64,128]{1,0:T(8,128)S(1)} %get-tuple-element.19), channel_id=1, source_target_pairs={{0,17},{1,16},{2,19},{3,18},{4,21},{5,20},{6,23},{7,22},{8,25},{9,... | collective-permute-start | bytes 98312 | tf_op jit(solution)/shard_map/ppermute | solution.py:219
  8.3 1.6 %collective-permute-start.1 = (f32[64,128]{1,0:T(8,128)S(1)}, f32[64,128]{1,0:T(8,128)S(1)}, u32[]{:S(2)}, u32[]{:S(2)}) collective-permute-start(f32[64,128]{1,0:T(8,128)S(1)} %get-tuple-element.19), channel_id=1, source_target_pairs={{0,16},{1,17},{2,18},{3,19},{4,20},{5,21},{6,22},{7,23},{8,24},{9,... | collective-permute-start | bytes 98312 | tf_op jit(solution)/shard_map/ppermute | solution.py:219
  9.8 0.0 collective-permute-start
  9.8 0.0 collective-permute-done.2
  9.9 2.0 %collective-permute-done.1 = f32[64,128]{1,0:T(8,128)S(1)} collective-permute-done((f32[64,128]{1,0:T(8,128)S(1)}, f32[64,128]{1,0:T(8,128)S(1)}, u32[]{:S(2)}, u32[]{:S(2)}) %collective-permute-start.1) | collective-permute-done | bytes 32800 | tf_op jit(solution)/shard_map/ppermute | solution.py:219
  11.8 0.0 collective-permute-done
  11.9 2.1 %collective-permute-start.5 = (f32[64,128]{1,0:T(8,128)S(1)}, f32[64,128]{1,0:T(8,128)S(1)}, u32[]{:S(2)}, u32[]{:S(2)}) collective-permute-start(f32[64,128]{1,0:T(8,128)S(1)} %add_add_fusion.3), channel_id=1, source_target_pairs={{0,6},{1,7},{2,4},{3,5},{4,2},{5,3},{6,0},{7,1},{8,14},{9,15},{10,... | collective-permute-start | bytes 98312 | tf_op jit(solution)/shard_map/ppermute | solution.py:219
  14.0 0.5 collective-permute-start.4
  14.5 0.7 collective-permute-start.3
  15.2 0.7 collective-permute-done.5
  15.9 2.3 %collective-permute-done.4 = f32[64,128]{1,0:T(8,128)S(1)} collective-permute-done((f32[64,128]{1,0:T(8,128)S(1)}, f32[64,128]{1,0:T(8,128)S(1)}, u32[]{:S(2)}, u32[]{:S(2)}) %collective-permute-start.4) | collective-permute-done | bytes 32800 | tf_op jit(solution)/shard_map/ppermute | solution.py:219
  18.2 0.0 collective-permute-done.3
  18.2 2.8 %collective-permute-start.8 = (f32[64,128]{1,0:T(8,128)S(1)}, f32[64,128]{1,0:T(8,128)S(1)}, u32[]{:S(2)}, u32[]{:S(2)}) collective-permute-start(f32[64,128]{1,0:T(8,128)S(1)} %add_add_fusion.2), channel_id=1, source_target_pairs={{0,136},{1,137},{2,138},{3,139},{4,140},{5,141},{6,142},{7,143},{8... | collective-permute-start | bytes 98312 | tf_op jit(solution)/shard_map/ppermute | solution.py:219
  21.1 0.3 collective-permute-start.7
  21.4 0.3 collective-permute-start.6
  21.7 3.1 %near_step.1 = (f32[64,512]{1,0:T(8,128)S(1)}, f32[4,64,512]{2,1,0:T(8,128)S(1)}, s32[64,512]{1,0:T(8,128)S(1)}, bf16[64,64,512]{2,1,0:T(8,128)(2,1)S(1)}, f32[8...) custom-call(s32[1]{0:T(128)S(6)} %copy.13.count_ref, s32[1,512]{1,0:T(1,128)} %bitcast.21, f32[64,512]{1,0:T(8,128)} %bitcast.17, ...), custom_call_target="tpu_custom_call" | custom-call | tf_op jit(solution)/shard_map/near_step/pallas_call | solution.py:247
  24.9 0.0 collective-permute-done.8
  24.9 0.5 collective-permute-done.7
  25.3 0.0 collective-permute-done.6
  25.4 5.2 %collective-permute-start.11 = (f32[64,128]{1,0:T(8,128)S(1)}, f32[64,128]{1,0:T(8,128)S(1)}, u32[]{:S(2)}, u32[]{:S(2)}) collective-permute-start(f32[64,128]{1,0:T(8,128)S(1)} %add_add_fusion.1), channel_id=1, source_target_pairs={{0,96},{1,97},{2,98},{3,99},{4,100},{5,101},{6,102},{7,103},{8,104... | collective-permute-start | bytes 98312 | tf_op jit(solution)/shard_map/ppermute | solution.py:219
  30.6 1.2 %collective-permute-start.10 = (f32[64,128]{1,0:T(8,128)S(1)}, f32[64,128]{1,0:T(8,128)S(1)}, u32[]{:S(2)}, u32[]{:S(2)}) collective-permute-start(f32[64,128]{1,0:T(8,128)S(1)} %add_add_fusion.1), channel_id=1, source_target_pairs={{0,64},{1,65},{2,66},{3,67},{4,68},{5,69},{6,70},{7,71},{8,72},{9,... | collective-permute-start | bytes 98312 | tf_op jit(solution)/shard_map/ppermute | solution.py:219
  31.7 1.0 %collective-permute-start.9 = (f32[64,128]{1,0:T(8,128)S(1)}, f32[64,128]{1,0:T(8,128)S(1)}, u32[]{:S(2)}, u32[]{:S(2)}) collective-permute-start(f32[64,128]{1,0:T(8,128)S(1)} %add_add_fusion.1), channel_id=1, source_target_pairs={{0,32},{1,33},{2,34},{3,35},{4,36},{5,37},{6,38},{7,39},{8,40},{9,... | collective-permute-start | bytes 98312 | tf_op jit(solution)/shard_map/ppermute | solution.py:219
  32.7 0.0 collective-permute-done.11
  32.7 4.7 %collective-permute-done.10 = f32[64,128]{1,0:T(8,128)S(1)} collective-permute-done((f32[64,128]{1,0:T(8,128)S(1)}, f32[64,128]{1,0:T(8,128)S(1)}, u32[]{:S(2)}, u32[]{:S(2)}) %collective-permute-start.10) | collective-permute-done | bytes 32800 | tf_op jit(solution)/shard_map/ppermute | solution.py:219
  37.4 0.0 collective-permute-done.9
  37.4 2.5 %residual_step.1 = (f32[4,64]{1,0:T(4,128)}, f32[64,512]{1,0:T(8,128)}, f32[1280,128]{1,0:T(8,128)S(1)}) custom-call(f32[64,128]{1,0:T(8,128)S(1)} %add_add_fusion.sums_ref, f32[64,512]{1,0:T(8,128)S(1)} %get-tuple-element.22.live_ref, f32[4,64,512]{2,1,0:T(8,128)S(1)} %get-tuple-element.23.ap_ref, s32[64,512]{1,0:T(8,128)S(1)} %get-tuple-element.24.seg_ref, ...), custom_call_target="tpu_custom_call" | custom-call | tf_op jit(solution)/shard_map/residual_step/pallas_call | solution.py:269
  39.9 35.6 %all_to_all.5 = f32[256,1,640]{2,1,0:T(1,128)S(1)} all-to-all(f32[256,1,640]{2,1,0:T(1,128)S(1)} %bitcast.11), channel_id=1, replica_groups=mesh['grp'=16,'mem'=16] {'grp','mem'}, dimensions={0} | all-to-all | bytes 1310720 | tf_op jit(solution)/shard_map/all_to_all | solution.py:282
  75.5 1.1 %calibration_step.1 = f32[64,64]{1,0:T(8,128)} custom-call(f32[1280,128]{1,0:T(8,128)S(1)} %bitcast.10), custom_call_target="tpu_custom_call" | custom-call | tf_op jit(solution)/shard_map/calibration_step/pallas_call | solution.py:283
  (4 shorter events, 0.0 us)
Async XLA Ops:
  5.1 4.7 %collective-permute-start.2 = (f32[64,128]{1,0:T(8,128)S(1)}, f32[64,128]{1,0:T(8,128)S(1)}, u32[]{:S(2)}, u32[]{:S(2)}) collective-permute-start(f32[64,128]{1,0:T(8,128)S(1)} %get-tuple-element.19), channel_id=1, source_target_pairs={{0,17},{1,16},{2,19},{3,18},{4,21},{5,20},{6,23},{7,22},{8,25},{9,... | collective-permute-start | bytes 98312 | tf_op jit(solution)/shard_map/ppermute | solution.py:219
  8.3 3.6 %collective-permute-start.1 = (f32[64,128]{1,0:T(8,128)S(1)}, f32[64,128]{1,0:T(8,128)S(1)}, u32[]{:S(2)}, u32[]{:S(2)}) collective-permute-start(f32[64,128]{1,0:T(8,128)S(1)} %get-tuple-element.19), channel_id=1, source_target_pairs={{0,16},{1,17},{2,18},{3,19},{4,20},{5,21},{6,22},{7,23},{8,24},{9,... | collective-permute-start | bytes 98312 | tf_op jit(solution)/shard_map/ppermute | solution.py:219
  9.8 2.0 %collective-permute-start = (f32[64,128]{1,0:T(8,128)S(1)}, f32[64,128]{1,0:T(8,128)S(1)}, u32[]{:S(2)}, u32[]{:S(2)}) collective-permute-start(f32[64,128]{1,0:T(8,128)S(1)} %get-tuple-element.19), channel_id=1, source_target_pairs={{0,1},{1,0},{2,3},{3,2},{4,5},{5,4},{6,7},{7,6},{8,9},{9,8},{10,11... | collective-permute-start | bytes 98312 | tf_op jit(solution)/shard_map/ppermute | solution.py:219
  11.9 4.1 %collective-permute-start.5 = (f32[64,128]{1,0:T(8,128)S(1)}, f32[64,128]{1,0:T(8,128)S(1)}, u32[]{:S(2)}, u32[]{:S(2)}) collective-permute-start(f32[64,128]{1,0:T(8,128)S(1)} %add_add_fusion.3), channel_id=1, source_target_pairs={{0,6},{1,7},{2,4},{3,5},{4,2},{5,3},{6,0},{7,1},{8,14},{9,15},{10,... | collective-permute-start | bytes 98312 | tf_op jit(solution)/shard_map/ppermute | solution.py:219
  14.0 4.3 %collective-permute-start.4 = (f32[64,128]{1,0:T(8,128)S(1)}, f32[64,128]{1,0:T(8,128)S(1)}, u32[]{:S(2)}, u32[]{:S(2)}) collective-permute-start(f32[64,128]{1,0:T(8,128)S(1)} %add_add_fusion.3), channel_id=1, source_target_pairs={{0,4},{1,5},{2,6},{3,7},{4,0},{5,1},{6,2},{7,3},{8,12},{9,13},{10,... | collective-permute-start | bytes 98312 | tf_op jit(solution)/shard_map/ppermute | solution.py:219
  14.5 3.8 %collective-permute-start.3 = (f32[64,128]{1,0:T(8,128)S(1)}, f32[64,128]{1,0:T(8,128)S(1)}, u32[]{:S(2)}, u32[]{:S(2)}) collective-permute-start(f32[64,128]{1,0:T(8,128)S(1)} %add_add_fusion.3), channel_id=1, source_target_pairs={{0,2},{1,3},{2,0},{3,1},{4,6},{5,7},{6,4},{7,5},{8,10},{9,11},{10,... | collective-permute-start | bytes 98312 | tf_op jit(solution)/shard_map/ppermute | solution.py:219
  18.2 6.6 %collective-permute-start.8 = (f32[64,128]{1,0:T(8,128)S(1)}, f32[64,128]{1,0:T(8,128)S(1)}, u32[]{:S(2)}, u32[]{:S(2)}) collective-permute-start(f32[64,128]{1,0:T(8,128)S(1)} %add_add_fusion.2), channel_id=1, source_target_pairs={{0,136},{1,137},{2,138},{3,139},{4,140},{5,141},{6,142},{7,143},{8... | collective-permute-start | bytes 98312 | tf_op jit(solution)/shard_map/ppermute | solution.py:219
  21.1 4.3 %collective-permute-start.7 = (f32[64,128]{1,0:T(8,128)S(1)}, f32[64,128]{1,0:T(8,128)S(1)}, u32[]{:S(2)}, u32[]{:S(2)}) collective-permute-start(f32[64,128]{1,0:T(8,128)S(1)} %add_add_fusion.2), channel_id=1, source_target_pairs={{0,8},{1,9},{2,10},{3,11},{4,12},{5,13},{6,14},{7,15},{8,0},{9,1},... | collective-permute-start | bytes 98312 | tf_op jit(solution)/shard_map/ppermute | solution.py:219
  21.4 3.9 %collective-permute-start.6 = (f32[64,128]{1,0:T(8,128)S(1)}, f32[64,128]{1,0:T(8,128)S(1)}, u32[]{:S(2)}, u32[]{:S(2)}) collective-permute-start(f32[64,128]{1,0:T(8,128)S(1)} %add_add_fusion.2), channel_id=1, source_target_pairs={{0,128},{1,129},{2,130},{3,131},{4,132},{5,133},{6,134},{7,135},{8... | collective-permute-start | bytes 98312 | tf_op jit(solution)/shard_map/ppermute | solution.py:219
  25.4 7.4 %collective-permute-start.11 = (f32[64,128]{1,0:T(8,128)S(1)}, f32[64,128]{1,0:T(8,128)S(1)}, u32[]{:S(2)}, u32[]{:S(2)}) collective-permute-start(f32[64,128]{1,0:T(8,128)S(1)} %add_add_fusion.1), channel_id=1, source_target_pairs={{0,96},{1,97},{2,98},{3,99},{4,100},{5,101},{6,102},{7,103},{8,104... | collective-permute-start | bytes 98312 | tf_op jit(solution)/shard_map/ppermute | solution.py:219
  30.6 6.8 %collective-permute-start.10 = (f32[64,128]{1,0:T(8,128)S(1)}, f32[64,128]{1,0:T(8,128)S(1)}, u32[]{:S(2)}, u32[]{:S(2)}) collective-permute-start(f32[64,128]{1,0:T(8,128)S(1)} %add_add_fusion.1), channel_id=1, source_target_pairs={{0,64},{1,65},{2,66},{3,67},{4,68},{5,69},{6,70},{7,71},{8,72},{9,... | collective-permute-start | bytes 98312 | tf_op jit(solution)/shard_map/ppermute | solution.py:219
  31.7 5.7 %collective-permute-start.9 = (f32[64,128]{1,0:T(8,128)S(1)}, f32[64,128]{1,0:T(8,128)S(1)}, u32[]{:S(2)}, u32[]{:S(2)}) collective-permute-start(f32[64,128]{1,0:T(8,128)S(1)} %add_add_fusion.1), channel_id=1, source_target_pairs={{0,32},{1,33},{2,34},{3,35},{4,36},{5,37},{6,38},{7,39},{8,40},{9,... | collective-permute-start | bytes 98312 | tf_op jit(solution)/shard_map/ppermute | solution.py:219
